TPU v7x, 32 devices: a whole 2x2x4 slice. The times are simulated.
32 devices in a mesh: groups: 2 (over x), tensor: 16 (over z, y, core).
Axes of the slice: x: 2, y: 2, z: 4, core: 2. Of those that a mesh axis runs over, the one named last changes fastest.
Arguments:
- input_rows: bfloat16 [512, 8192], P(('groups', 'tensor')), parts along dimension 0, may hold values from -6 to 6
- up_weight: bfloat16 [8192, 28672], P(None, 'tensor'), may hold values from -0.0625 to 0.0625
- adapter_down: bfloat16 [32, 64, 8192], P(('groups', 'tensor')), parts along dimension 0, may hold values from -0.0625 to 0.0625
- adapter_up: bfloat16 [32, 64, 28672], P(('groups', 'tensor')), parts along dimension 0, may hold values from -0.75 to 0.75
- ranks: int32 [32], P('groups'), parts along dimension 0, may hold values from 16 to 64, as said below
- adapter_slot: int32 [32], P('groups'), parts along dimension 0, may hold values from 0 to 15, each once
- segment_lengths: int32 [32], P('groups'), parts along dimension 0, may hold values from 1 to 64, 256 in all
- segment_adapter: int32 [32], P('groups'), parts along dimension 0, may hold values from 0 to 15
Outputs:
- up_out: bfloat16 [512, 28672], P('groups', 'tensor'), parts along dimension 0
There are 2 independent parts, one for each index of `groups`. A program takes and returns all parts, laid end to end along the dimension named above; an argument that names none is the same for every part. Nothing has to cross between parts.
Inputs may be any that keep to these rules, and one draw needn't show every extreme that they name: `ranks`: a multiple of 16; the columns j >= the rank of an adapter's 64 are unused. `adapter_slot`: each storage slot holds exactly one adapter. `segment_lengths`: the segments sum to 256.
All inputs are finite; a program needn't handle non-finite values.
Results may differ from a plain program's by a relative error of at most 0.0039.
Values may be sent and summed in bfloat16 or wider, within the bound.
No kernel may reach another device: no remote copies, remote signals or barrier semaphores. Data moves between devices by JAX's collectives and lax.ppermute only.
A program may use at most 128 MiB of HBM per device.

v0:
```python
import jax
import jax.numpy as jnp
import numpy as np
from jax import lax
from jax.experimental import pallas as pl
from jax.experimental.pallas import tpu as pltpu
from jax.sharding import PartitionSpec as P

ADAPTER_ALPHA = 32.0
POOLED_SHARDS = 16
FIRST_ROWS = 64
MORE_ROWS = (16, 32)
WIDE_GRANT = 56 << 20


def row_tables(row_count, ranks, adapter_slot, segment_lengths, segment_adapter):
    seg_ends = jnp.cumsum(segment_lengths)
    positions = jnp.arange(row_count, dtype=jnp.int32)
    seg_row = jnp.sum((seg_ends[None, :] <= positions[:, None]).astype(jnp.int32), axis=1)
    seg_pick = (
        seg_row[:, None] == jnp.arange(segment_lengths.shape[0], dtype=jnp.int32)[None, :]
    ).astype(jnp.int32)
    adapter_row = jnp.sum(seg_pick * segment_adapter[None, :], axis=1)
    pool_pick = (
        adapter_row[:, None] == jnp.arange(ranks.shape[0], dtype=jnp.int32)[None, :]
    ).astype(jnp.int32)
    slot_row = jnp.sum(pool_pick * adapter_slot[None, :], axis=1)
    row_rank_values = jnp.sum(pool_pick * ranks[None, :], axis=1)
    return (slot_row, row_rank_values)


def vmem(buffers):
    return pltpu.CompilerParams(vmem_limit_bytes=buffers + (8 << 20))


def split_for_pair(up_factor, down_factor, core, chips):
    rank_width, hidden = up_factor.shape
    width = hidden // (2 * chips)
    features = down_factor.shape[1] // 2

    def kernel(core_ref, source, down, mine, other, half_down, sems):
        core = core_ref[0]
        start = pl.multiple_of((1 - core) * features, features)
        copies = [
            pltpu.make_async_copy(
                down.at[:, pl.ds(start, features)], half_down, sems.at[2 * chips]
            )
        ]
        for q in range(chips):
            for i, (target, half) in enumerate(((other, 1 - core), (mine, core))):
                start = pl.multiple_of((2 * q + half) * width, width)
                copies.append(
                    pltpu.make_async_copy(
                        source.at[:, pl.ds(start, width)], target.at[q], sems.at[2 * q + i]
                    )
                )
        for copy in copies:
            copy.start()
        for copy in copies:
            copy.wait()

    block = jax.ShapeDtypeStruct((chips, rank_width, width), up_factor.dtype)
    return pl.pallas_call(
        kernel,
        in_specs=[pl.BlockSpec(memory_space=pltpu.SMEM)]
        + [pl.BlockSpec(memory_space=pltpu.HBM)] * 2,
        out_specs=[pl.BlockSpec(memory_space=pltpu.VMEM)] * 3,
        out_shape=[
            block, block, jax.ShapeDtypeStruct((rank_width, features), down_factor.dtype)
        ],
        scratch_shapes=[pltpu.SemaphoreType.DMA((2 * chips + 1,))],
        compiler_params=pltpu.CompilerParams(vmem_limit_bytes=WIDE_GRANT),
        cost_estimate=pl.CostEstimate(
            flops=0, bytes_accessed=4 * rank_width * hidden, transcendentals=0
        ),
    )(core, up_factor, down_factor)


def describe(ranks, adapter_slot, segment_lengths, segment_adapter, position, total_rows, limit):
    slots, segments = ranks.shape[0], segment_lengths.shape[0]
    rank_width = limit // 2
    shift = rank_width.bit_length() - 1

    def kernel(
        ranks_in, home_in, length_in, adapter_in, position_ref,
        gain_ref, own_ref, choose_ref, live_ref, fixed_ref, code_ref, begin_ref, full_ref,
        rank_of, rows_of, used, factor, order, ranks_ref, home_ref, length_ref, adapter_ref, sems,
    ):
        pairs = zip(
            (ranks_in, home_in, length_in, adapter_in),
            (ranks_ref, home_ref, length_ref, adapter_ref),
        )
        copies = [
            pltpu.make_async_copy(source, target, sems.at[i])
            for i, (source, target) in enumerate(pairs)
        ]
        for copy in copies:
            copy.start()
        for copy in copies:
            copy.wait()
        for a in range(slots):
            rows_of[a] = 0
            rank_of[home_ref[a]] = ranks_ref[a]
        starts, start = [], jnp.int32(0)
        for i in range(segments):
            slot = home_ref[adapter_ref[i]]
            starts.append((start, start + length_ref[i], slot))
            order[i] = rows_of[slot] - start
            rows_of[slot] = rows_of[slot] + length_ref[i]
            start = start + length_ref[i]
        full = jnp.int32(0)
        for s in range(slots):
            used[s] = jnp.minimum(rows_of[s], rank_of[s])
            factor[s] = (rank_of[s] < rows_of[s]).astype(jnp.int32)
            begin_ref[s] = used[s - 1] if s % 2 else jnp.int32(0)
            if s % 2:
                full = jnp.maximum(full, used[s - 1] + used[s])
        full_ref[0] = full

        def tables(row):
            spot, code = jnp.zeros_like(row), jnp.zeros_like(row)
            for i, (low, high, slot) in enumerate(starts):
                hit = (row >= low) & (row < high)
                spot = jnp.where(hit, row + (order[i] + begin_ref[slot]), spot)
                code = jnp.where(hit, slot + 32 * factor[slot] + 64 * rank_of[slot], code)
            return spot, code & 31, (code >> 5) & 1, code >> 6

        here = position_ref[0]
        spot, slot, by_factor, _ = tables(lax.broadcasted_iota(jnp.int32, (total_rows, limit), 0))
        code_ref[...] = slot + 32 * by_factor + 64 * spot

        lane = lax.broadcasted_iota(jnp.int32, (total_rows // 2, limit), 1)
        row = lax.broadcasted_iota(jnp.int32, (total_rows // 2, limit), 0)
        _, slot, _, rank = tables(row + (lane >> shift) * (total_rows // 2))
        own_ref[...] = jnp.where(slot == here, 1.0, 0.0)
        scale = ADAPTER_ALPHA / rank.astype(jnp.float32)
        inside = ((slot >> 1) == (here >> 1)) & ((lane & (rank_width - 1)) < rank)
        gain_ref[...] = jnp.where(inside, scale, 0.0)

        spot, slot, by_factor, _ = tables(lax.broadcasted_iota(jnp.int32, (8, total_rows), 1))
        mine = ((slot >> 1) == (here >> 1)) & (by_factor == 0)
        spot = jnp.broadcast_to(jnp.where(mine, spot, -1)[:1], (limit, total_rows))
        line = lax.broadcasted_iota(jnp.int32, (limit, total_rows), 0)
        choose_ref[...] = jnp.where(line == spot, 1.0, 0.0).astype(jnp.bfloat16)

        line = lax.broadcasted_iota(jnp.int32, (limit, limit), 0)
        lane = lax.broadcasted_iota(jnp.int32, (limit, limit), 1)
        half, column = lane >> shift, lane & (rank_width - 1)
        other = here ^ 1
        begin = jnp.where(half == 0, begin_ref[here], begin_ref[other])
        many = jnp.where(half == 0, used[here], used[other])
        kind = jnp.where(half == 0, factor[here], factor[other])
        held = (line == begin + column) & (column < many) & (kind == 1)
        fixed_ref[...] = jnp.where(held, 1.0, 0.0).astype(jnp.bfloat16)
        live = (line >= begin) & (line < begin + many) & (kind == 0)
        live_ref[...] = jnp.where(live, 1.0, 0.0)

    smem, whole = pl.BlockSpec(memory_space=pltpu.SMEM), pl.BlockSpec(memory_space=pltpu.VMEM)
    return pl.pallas_call(
        kernel,
        in_specs=[pl.BlockSpec(memory_space=pltpu.HBM)] * 4 + [smem],
        out_specs=[whole] * 6 + [smem] * 2,
        out_shape=[
            jax.ShapeDtypeStruct((total_rows // 2, limit), jnp.float32),
            jax.ShapeDtypeStruct((total_rows // 2, limit), jnp.float32),
            jax.ShapeDtypeStruct((limit, total_rows), jnp.bfloat16),
            jax.ShapeDtypeStruct((limit, limit), jnp.float32),
            jax.ShapeDtypeStruct((limit, limit), jnp.bfloat16),
            jax.ShapeDtypeStruct((total_rows, limit), jnp.int32),
            jax.ShapeDtypeStruct((slots,), jnp.int32),
            jax.ShapeDtypeStruct((1,), jnp.int32),
        ],
        scratch_shapes=[pltpu.SMEM((slots,), jnp.int32)] * 4
        + [pltpu.SMEM((segments,), jnp.int32)]
        + [pltpu.SMEM((slots,), jnp.int32)] * 2
        + [pltpu.SMEM((segments,), jnp.int32)] * 2
        + [pltpu.SemaphoreType.DMA((4,))],
        compiler_params=vmem(16 * total_rows * limit),
        cost_estimate=pl.CostEstimate(
            flops=200 * total_rows * limit, bytes_accessed=16 * total_rows * limit, transcendentals=0
        ),
    )(ranks, adapter_slot, segment_lengths, segment_adapter, position)


def collect_rows(blocks, places, core, own_down, other_down, own):
    count = len(blocks)
    height, features = blocks[0].shape
    height = height // 2
    rank_width = other_down.shape[0]
    half_rows = own.shape[0]
    chunk = 1024 if features % 1024 == 0 else features
    chunks = features // chunk

    def kernel(places_ref, core_ref, own_ref, *refs):
        sources, own_down_ref, other_down_ref = refs[:count], refs[count], refs[count + 1]
        rows_ref, shrink_ref, downs, sems = refs[count + 2 :]
        groups = []
        for k in range(chunks):
            columns = pl.ds(k * chunk, chunk)
            offset = pl.multiple_of(core_ref[0] * features + k * chunk, chunk)
            copies = [
                pltpu.make_async_copy(
                    own_down_ref.at[:, pl.ds(offset, chunk)],
                    downs.at[pl.ds(0, rank_width), columns],
                    sems.at[k, 2 * count],
                ),
                pltpu.make_async_copy(
                    other_down_ref.at[:, columns],
                    downs.at[pl.ds(rank_width, rank_width), columns],
                    sems.at[k, 2 * count + 1],
                ),
            ]
            for i in range(2 * count):
                start = pl.multiple_of(places_ref[i] * height, height)
                copies.append(
                    pltpu.make_async_copy(
                        sources[i // 2].at[pl.ds(i % 2 * height, height), columns],
                        rows_ref.at[pl.ds(start, height), columns],
                        sems.at[k, i],
                    )
                )
            groups.append(copies)
            for copy in copies:
                copy.start()
        shrink = jnp.zeros((2 * half_rows, 2 * rank_width), jnp.float32)
        for k in range(chunks):
            for copy in groups[k]:
                copy.wait()
            columns = pl.ds(k * chunk, chunk)
            shrink = shrink + lax.dot_general(
                rows_ref[:, columns],
                downs[:, columns],
                (((1,), (1,)), ((), ())),
                preferred_element_type=jnp.float32,
            )
        top, bottom = shrink[:half_rows], shrink[half_rows:]
        first = jnp.concatenate([top[:, :rank_width], bottom[:, :rank_width]], axis=1)
        second = jnp.concatenate([top[:, rank_width:], bottom[:, rank_width:]], axis=1)
        shrink_ref[...] = jnp.where(own_ref[...] > 0.5, first, second)

    smem, whole = pl.BlockSpec(memory_space=pltpu.SMEM), pl.BlockSpec(memory_space=pltpu.VMEM)
    rows = 2 * count * height
    return pl.pallas_call(
        kernel,
        in_specs=[smem, smem, whole] + [pl.BlockSpec(memory_space=pl.ANY)] * (count + 2),
        out_specs=[whole] * 2,
        out_shape=[
            jax.ShapeDtypeStruct((rows, features), blocks[0].dtype),
            jax.ShapeDtypeStruct(own.shape, jnp.float32),
        ],
        scratch_shapes=[
            pltpu.VMEM((2 * rank_width, features), own_down.dtype),
            pltpu.SemaphoreType.DMA((chunks, 2 * count + 2)),
        ],
        compiler_params=pltpu.CompilerParams(vmem_limit_bytes=WIDE_GRANT),
        cost_estimate=pl.CostEstimate(
            flops=4 * rows * features * rank_width,
            bytes_accessed=4 * rows * features,
            transcendentals=0,
        ),
    )(places, core, own, *blocks, own_down, other_down)


def build_payload(choose, live, fixed, coeff, mine, other, first, count):
    chips, rank_width, width = mine.shape

    half_rows = coeff.shape[0]

    def kernel(choose_ref, live_ref, fixed_ref, coeff_ref, mine_ref, other_ref, out_ref):
        lines = pl.ds(first, count)
        folded = coeff_ref[...]
        top = jnp.dot(choose_ref[lines, :half_rows], folded, preferred_element_type=jnp.float32)
        low = jnp.dot(choose_ref[lines, half_rows:], folded, preferred_element_type=jnp.float32)
        chosen = top[:, :rank_width] + low[:, rank_width:]
        select = jnp.concatenate([chosen, chosen], axis=1) * live_ref[lines]
        select = (select + fixed_ref[lines].astype(jnp.float32)).astype(jnp.bfloat16)

        @pl.loop(0, chips)
        def _(q):
            out_ref[q] = jnp.dot(
                select,
                jnp.concatenate([mine_ref[q], other_ref[q]], axis=0),
                preferred_element_type=jnp.float32,
            ).astype(out_ref.dtype)

    return pl.pallas_call(
        kernel,
        in_specs=[pl.BlockSpec(memory_space=pltpu.VMEM)] * 6,
        out_specs=pl.BlockSpec(memory_space=pltpu.VMEM),
        out_shape=jax.ShapeDtypeStruct((chips, count, width), mine.dtype),
        compiler_params=vmem(4 * chips * width * (2 * rank_width + count)),
        cost_estimate=pl.CostEstimate(
            flops=4 * chips * count * rank_width * width,
            bytes_accessed=2 * chips * width * (2 * rank_width + count),
            transcendentals=0,
        ),
    )(choose, live, fixed, coeff, mine, other)


def combine(base, code, begin, more, coeff, incoming, extra):
    total_rows, width = base.shape
    chips, first, _ = incoming.shape
    second = extra.shape[1]
    limit = first + second
    rank_width = limit // 2
    shift = rank_width.bit_length() - 1
    tile = 256 if width % 256 == 0 else 128

    def kernel(
        begin_ref, more_ref, base_ref, code_ref, coeff_ref, incoming_ref, extra_ref,
        out_ref, late, base_part, near_rows, sems,
    ):
        fetch = pltpu.make_async_copy(extra_ref, late, sems.at[0])
        get_base = pltpu.make_async_copy(base_ref, base_part, sems.at[1])
        get_near = pltpu.make_async_copy(incoming_ref, near_rows, sems.at[2])
        get_near.start()
        get_base.start()
        folded = coeff_ref[...].astype(jnp.float32)
        both = jnp.concatenate(
            [
                jnp.concatenate([part, part], axis=1)
                for part in (folded[:, :rank_width], folded[:, rank_width:])
            ],
            axis=0,
        )
        code_value = code_ref[...]
        slot, by_factor, spot = code_value & 31, (code_value >> 5) & 1, code_value >> 6
        lane = lax.broadcasted_iota(jnp.int32, (total_rows, limit), 1)
        owned = jnp.where(by_factor == 1, slot, -1) - (lane >> shift)
        finished = jnp.where(by_factor == 0, spot, -1)[:, :1]
        finished_chip = (slot >> 1)[:, :1]

        def weights(low, count):
            target = finished - low
            target = jnp.where((target >= 0) & (target < count), finished_chip * count + target, -1)
            wide = lax.broadcasted_iota(jnp.int32, (total_rows, chips * count), 1)
            total = jnp.where(wide == target, 1.0, 0.0)
            line = lax.broadcasted_iota(jnp.int32, (limit, chips * count), 0)
            place = lax.broadcasted_iota(jnp.int32, (limit, chips * count), 1)
            for q in range(chips):
                goal = jnp.where(
                    line < rank_width, line, line - rank_width + begin_ref[2 * q + 1]
                ) - low
                moved = (goal >= 0) & (goal < count) & (place == q * count + goal)
                moved = jnp.where(moved, 1.0, 0.0).astype(jnp.bfloat16)
                part = jnp.where(owned == 2 * q, both, 0.0).astype(jnp.bfloat16)
                total = total + jnp.dot(part, moved, preferred_element_type=jnp.float32)
            return total.astype(jnp.bfloat16)

        near = weights(0, first)
        get_near.wait()
        get_base.wait()

        def write(far):
            @pl.loop(0, width // tile)
            def _(i):
                columns = pl.ds(pl.multiple_of(i * tile, tile), tile)
                block = near_rows[:, :, columns].reshape(chips * first, tile)
                total = jnp.dot(near, block, preferred_element_type=jnp.float32)
                total += base_part[:, columns]
                if far is not None:
                    block = late[:, :, columns].reshape(chips * second, tile)
                    total += jnp.dot(far, block, preferred_element_type=jnp.float32)
                out_ref[:, columns] = total.astype(out_ref.dtype)

        @pl.when(more_ref[0] > first)
        def _():
            fetch.start()
            far = weights(first, second)
            fetch.wait()
            write(far)

        @pl.when(more_ref[0] <= first)
        def _():
            write(None)

    smem, whole = pl.BlockSpec(memory_space=pltpu.SMEM), pl.BlockSpec(memory_space=pltpu.VMEM)
    return pl.pallas_call(
        kernel,
        in_specs=[smem] * 2
        + [pl.BlockSpec(memory_space=pl.ANY)]
        + [whole] * 2
        + [pl.BlockSpec(memory_space=pl.ANY)] * 2,
        out_specs=whole,
        out_shape=jax.ShapeDtypeStruct((total_rows, width), jnp.bfloat16),
        scratch_shapes=[
            pltpu.VMEM(extra.shape, extra.dtype),
            pltpu.VMEM(base.shape, base.dtype),
            pltpu.VMEM(incoming.shape, incoming.dtype),
            pltpu.SemaphoreType.DMA((3,)),
        ],
        compiler_params=vmem(8 * total_rows * width + 2 * chips * limit * width),
        cost_estimate=pl.CostEstimate(
            flops=4 * total_rows * chips * limit * width,
            bytes_accessed=6 * total_rows * width + 2 * chips * limit * width,
            transcendentals=0,
        ),
    )(begin, more, base, code, coeff, incoming, extra)


def ring_gather(block, shards, halfway):
    chips = shards // 2
    depth = chips // 2
    cycle = list(range(0, chips, 2)) + list(range(chips - 1, 0, -2))
    ahead = [
        (2 * cycle[p] + c, 2 * cycle[(p + 1) % chips] + c) for p in range(chips) for c in range(2)
    ]
    back = [(b, a) for a, b in ahead]
    held = {0: block}
    for step in range(1, depth + 1):
        held[-step] = lax.ppermute(held[1 - step], "tensor", ahead)
        if step < chips - depth:
            held[step] = lax.ppermute(held[step - 1], "tensor", back)
        held[-step] = halfway(step, held[-step])
    table = np.zeros((shards, shards), np.int32)
    for t in range(shards):
        for i, offset in enumerate(held):
            chip = cycle[(cycle.index(t // 2) + offset) % chips]
            table[t, 2 * i], table[t, 2 * i + 1] = 2 * chip + t % 2, 2 * chip + 1 - t % 2
    places = lax.dynamic_index_in_dim(table, lax.axis_index("tensor"), keepdims=False)
    return list(held.values()), places


def largest_over_groups(value):
    groups = lax.axis_size("groups")
    for shift in range(1, groups):
        other = lax.ppermute(value, "groups", [(g, (g + shift) % groups) for g in range(groups)])
        value = jnp.maximum(value, other)
    return value


def pooled(
    input_rows,
    up_weight,
    adapter_down,
    adapter_up,
    ranks,
    adapter_slot,
    segment_lengths,
    segment_adapter,
):
    shards = lax.axis_size("tensor")
    position = lax.axis_index("tensor").astype(jnp.int32)
    chips = shards // 2
    total_rows = input_rows.shape[0] * shards
    rank_width = adapter_up.shape[1]
    limit = 2 * rank_width
    sibling = [(t, t ^ 1) for t in range(shards)]
    same_core = [list(range(c, shards, 2)) for c in range(2)]

    core = position & 1
    features = input_rows.shape[1] // 2

    def swap(value):
        keep = lax.dynamic_slice_in_dim(value, core * features, features, 1)
        send = lax.dynamic_slice_in_dim(value, (1 - core) * features, features, 1)
        return keep, lax.ppermute(send, "tensor", sibling)

    mine, other, down_half = split_for_pair(adapter_up[0], adapter_down[0], core[None], chips)
    block = jnp.concatenate(swap(input_rows), axis=0)
    block, mine, other, down_half = lax.optimization_barrier((block, mine, other, down_half))
    other = lax.ppermute(other, "tensor", sibling)
    down_half = lax.ppermute(down_half, "tensor", sibling)
    gain, own, choose, live, fixed, code, begin, full = describe(
        ranks, adapter_slot, segment_lengths, segment_adapter, position[None], total_rows, limit
    )
    fullest = largest_over_groups(full)
    pending = [(own, choose), (other, down_half)]

    def halfway(step, piece):
        nonlocal pending
        if step <= len(pending):
            piece, pending[step - 1] = lax.optimization_barrier((piece, pending[step - 1]))
        return piece

    blocks, places = ring_gather(block, shards, halfway)
    (own, choose), (other, down_half) = pending
    rows, shrink = collect_rows(blocks, places, core[None], adapter_down[0], down_half, own)
    shrink = shrink + lax.ppermute(shrink, "tensor", sibling)
    coeff = (shrink * gain).astype(jnp.bfloat16)
    coeff, rows, fullest = lax.optimization_barrier((coeff, rows, fullest))

    def payload(low, count):
        return build_payload(choose, live, fixed, coeff, mine, other, low, count)

    def exchange(value):
        return lax.all_to_all(
            value,
            "tensor",
            split_axis=0,
            concat_axis=0,
            axis_index_groups=same_core,
            tiled=True,
        )

    near = payload(0, FIRST_ROWS)
    rows_other = lax.ppermute(rows, "tensor", sibling)
    every, bit = coeff, 2
    while bit < shards:
        every = every + lax.ppermute(every, "tensor", [(t, t ^ bit) for t in range(shards)])
        if bit == 2:
            every, near = lax.optimization_barrier((every, near))
        bit *= 2
    near, every, rows, rows_other = lax.optimization_barrier((near, every, rows, rows_other))
    incoming = exchange(near)
    halves = [jnp.where(core == c, rows, rows_other) for c in range(2)]
    base = jnp.dot(
        jnp.concatenate(halves, axis=1), up_weight, preferred_element_type=jnp.float32
    )
    fullest, base, incoming = lax.optimization_barrier((fullest, base, incoming))
    rest = limit - FIRST_ROWS

    def later(count):
        def run():
            value = jnp.zeros((chips, rest - count, up_weight.shape[1]), adapter_up.dtype)
            if count:
                late = exchange(payload(FIRST_ROWS, count))
                value = jnp.concatenate([late, value], axis=1)
            return value

        return run

    sizes = (0,) + tuple(size for size in MORE_ROWS if size < rest) + (rest,)
    which = sum((fullest[0] > FIRST_ROWS + size).astype(jnp.int32) for size in sizes[:-1])
    extra = lax.switch(which, [later(size) for size in sizes])
    return combine(base, code, begin, fullest, every, incoming, extra)


def gathered(input_rows, up_weight, adapter_down, adapter_up, slot_row, row_rank):
    shards = lax.axis_size("tensor")
    position = lax.axis_index("tensor")
    total_rows = input_rows.shape[0] * shards
    stored, rank_width, hidden = adapter_up.shape
    width = hidden // shards
    slots = shards * stored
    outgoing = jnp.stack(
        [adapter_up[:, :, i * width : (i + 1) * width] for i in range(shards)], axis=0
    )
    incoming = lax.all_to_all(outgoing, "tensor", split_axis=0, concat_axis=0, tiled=True)
    rows = lax.all_gather(input_rows, "tensor", axis=0, tiled=True)
    shrink = jnp.einsum("gf,ojf->ogj", rows, adapter_down, preferred_element_type=jnp.float32)
    own = position * stored + jnp.arange(stored, dtype=jnp.int32)
    inside = jnp.arange(rank_width, dtype=jnp.int32)[None, :] < row_rank[:, None]
    keep = (slot_row[None, :] == own[:, None])[:, :, None] & inside[None]
    scale = ADAPTER_ALPHA / row_rank.astype(jnp.float32)
    own_coeff = jnp.where(keep, shrink * scale[None, :, None], 0.0).astype(jnp.bfloat16)
    base = jnp.dot(rows, up_weight, preferred_element_type=jnp.float32)
    own_coeff, base = lax.optimization_barrier((own_coeff, base))
    coeff = lax.all_gather(own_coeff, "tensor", axis=0, tiled=True)
    placed = coeff.transpose(1, 0, 2).reshape(total_rows, slots * rank_width)
    factors = incoming.reshape(slots * rank_width, width)
    term = jnp.dot(placed, factors, preferred_element_type=jnp.float32)
    return (base + term).astype(jnp.bfloat16)


def on_device(
    input_rows,
    up_weight,
    adapter_down,
    adapter_up,
    ranks,
    adapter_slot,
    segment_lengths,
    segment_adapter,
):
    shards = lax.axis_size("tensor")
    stored, rank_width, _ = adapter_up.shape
    tiled = up_weight.shape[1] % 128 == 0 and input_rows.shape[0] % 16 == 0 and rank_width == 64
    tiled = tiled and input_rows.shape[1] % 256 == 0 and input_rows.shape[0] * shards <= 256
    if shards == POOLED_SHARDS and stored == 1 and tiled:
        return pooled(
            input_rows,
            up_weight,
            adapter_down,
            adapter_up,
            ranks,
            adapter_slot,
            segment_lengths,
            segment_adapter,
        )
    slot_row, row_rank = row_tables(
        input_rows.shape[0] * shards, ranks, adapter_slot, segment_lengths, segment_adapter
    )
    return gathered(input_rows, up_weight, adapter_down, adapter_up, slot_row, row_rank)


def solution(mesh):
    placed = (
        P(("groups", "tensor"), None),
        P(None, "tensor"),
        P(("groups", "tensor"), None, None),
        P(("groups", "tensor"), None, None),
        P("groups"),
        P("groups"),
        P("groups"),
        P("groups"),
    )
    return jax.shard_map(
        on_device, mesh=mesh, in_specs=placed, out_specs=P("groups", "tensor"), check_vma=False
    )
```

profile of v0, /device:TPU:0, one launch (start us, length us, event | category | flops | bytes accessed | tf_op | source)
XLA Modules:
  0.0 115.6 jit_solution(3953400590158816471)
XLA Ops:
  0.0 1.0 constant_dynamic-slice_fusion.1
  1.5 3.7 %shard_map.92 = (bf16[8,64,1792]{2,1,0:T(8,128)(2,1)S(1)}, bf16[8,64,1792]{2,1,0:T(8,128)(2,1)}, bf16[64,4096]{1,0:T(8,128)(2,1)}) custom-call(s32[1]{0:T(128)} %bitcast.2.core_ref, bf16[64,28672]{1,0:T(8,128)(2,1)} %bitcast.10, bf16[64,8192]{1,0:T(8,128)(2,1)} %bitcast.8), custom_call_target="tpu_custom_call" | custom-call | bytes 7340032 | tf_op jit(solution)/shard_map/pallas_call | solution.py:63
  5.4 3.0 %collective-permute-start.1 = (bf16[32,4096]{1,0:T(8,128)(2,1)S(1)}, bf16[32,4096]{1,0:T(8,128)(2,1)S(1)}, u32[]{:S(2)}, u32[]{:S(2)}) collective-permute-start(bf16[32,4096]{1,0:T(8,128)(2,1)S(1)} %pad_maximum_fusion.refs_0_), channel_id=1, source_target_pairs={{0,4},{1,5},{4,8},{5,9},{8,12},{9,13},{12,14},{13,15},{14,10},{15,... | collective-permute-start | bytes 786440 | tf_op jit(solution)/shard_map/ppermute | solution.py:411
  8.5 2.1 %shard_map.91 = (f32[128,128]{1,0:T(8,128)S(1)}, f32[128,128]{1,0:T(8,128)S(1)}, bf16[128,256]{1,0:T(8,128)(2,1)S(1)}, f32[128,128]{1,0:T(8,128)S(1)}, bf16[128,...) custom-call(s32[16]{0:T(128)S(1)} %copy-done.1, s32[16]{0:T(128)S(1)} %copy-done.2, ...), custom_call_target="tpu_custom_call" | custom-call | flops 6553600 | bytes 524288 | tf_op jit(solution)/shard_map/pallas_call | solution.py:159
  11.3 3.6 %collective-permute-done.1.refs_1_ = bf16[32,4096]{1,0:T(8,128)(2,1)S(1)} collective-permute-done((bf16[32,4096]{1,0:T(8,128)(2,1)S(1)}, bf16[32,4096]{1,0:T(8,128)(2,1)S(1)}, u32[]{:S(2)}, u32[]{:S(2)}) %collective-permute-start.1) | collective-permute-done | bytes 262176 | tf_op jit(solution)/shard_map/ppermute | solution.py:411
  14.9 1.8 %collective-permute-start.3 = (bf16[32,4096]{1,0:T(8,128)(2,1)S(1)}, bf16[32,4096]{1,0:T(8,128)(2,1)S(1)}, u32[]{:S(2)}, u32[]{:S(2)}) collective-permute-start(bf16[32,4096]{1,0:T(8,128)(2,1)S(1)} %collective-permute-done.1.refs_1_), channel_id=1, source_target_pairs={{0,4},{1,5},{4,8},{5,9},{8,12},{9,13},{12,14},{13,15},{14,10},{15,... | collective-permute-start | bytes 786440 | tf_op jit(solution)/shard_map/ppermute | solution.py:411
  16.7 3.2 %collective-permute-done.2.refs_2_ = bf16[32,4096]{1,0:T(8,128)(2,1)S(1)} collective-permute-done((bf16[32,4096]{1,0:T(8,128)(2,1)S(1)}, bf16[32,4096]{1,0:T(8,128)(2,1)S(1)}, u32[]{:S(2)}, u32[]{:S(2)}) %collective-permute-start.2) | collective-permute-done | bytes 262176 | tf_op jit(solution)/shard_map/ppermute | solution.py:413
  20.2 2.5 %collective-permute-done.3.refs_3_ = bf16[32,4096]{1,0:T(8,128)(2,1)S(1)} collective-permute-done((bf16[32,4096]{1,0:T(8,128)(2,1)S(1)}, bf16[32,4096]{1,0:T(8,128)(2,1)S(1)}, u32[]{:S(2)}, u32[]{:S(2)}) %collective-permute-start.3) | collective-permute-done | bytes 262176 | tf_op jit(solution)/shard_map/ppermute | solution.py:411
  22.7 1.5 %collective-permute-start.7 = (bf16[32,4096]{1,0:T(8,128)(2,1)S(1)}, bf16[32,4096]{1,0:T(8,128)(2,1)}, u32[]{:S(2)}, u32[]{:S(2)}) collective-permute-start(bf16[32,4096]{1,0:T(8,128)(2,1)S(1)} %collective-permute-done.3.refs_3_), channel_id=1, source_target_pairs={{0,4},{1,5},{4,8},{5,9},{8,12},{9,13},{12,14},{13,15},{14,10},{15,... | collective-permute-start | bytes 786440 | tf_op jit(solution)/shard_map/ppermute | solution.py:411
  24.3 3.7 %collective-permute-done.6.refs_4_ = bf16[32,4096]{1,0:T(8,128)(2,1)} collective-permute-done((bf16[32,4096]{1,0:T(8,128)(2,1)S(1)}, bf16[32,4096]{1,0:T(8,128)(2,1)}, u32[]{:S(2)}, u32[]{:S(2)}) %collective-permute-start.6) | collective-permute-done | bytes 262176 | tf_op jit(solution)/shard_map/ppermute | solution.py:413
  28.4 1.4 %collective-permute-done.7.refs_5_ = bf16[32,4096]{1,0:T(8,128)(2,1)} collective-permute-done((bf16[32,4096]{1,0:T(8,128)(2,1)S(1)}, bf16[32,4096]{1,0:T(8,128)(2,1)}, u32[]{:S(2)}, u32[]{:S(2)}) %collective-permute-start.7) | collective-permute-done | bytes 262176 | tf_op jit(solution)/shard_map/ppermute | solution.py:411
  29.7 1.1 collective-permute-start.9
  30.9 1.2 %fusion.4.places_ref = s32[16]{0:T(128)} fusion(s32[16,16]{1,0:T(8,128)} %constant.36.clone, s32[]{:T(128)S(6)} %select_n.24), kind=kLoop, calls=%fused_computation.11 | loop fusion | bytes 132 | tf_op jit(solution)/shard_map/jit(dynamic_index_in_dim)/squeeze | solution.py:420
  32.1 3.2 %collective-permute-done.8.refs_6_ = bf16[32,4096]{1,0:T(8,128)(2,1)} collective-permute-done((bf16[32,4096]{1,0:T(8,128)(2,1)}, bf16[32,4096]{1,0:T(8,128)(2,1)}, u32[]{:S(2)}, u32[]{:S(2)}) %collective-permute-start.8) | collective-permute-done | bytes 262176 | tf_op jit(solution)/shard_map/ppermute | solution.py:413
  35.3 1.1 collective-permute-done.9.refs_7_
  36.4 5.3 %shard_map.93 = (bf16[256,4096]{1,0:T(8,128)(2,1)}, f32[128,128]{1,0:T(8,128)}) custom-call(s32[16]{0:T(128)} %fusion.4.places_ref, s32[1]{0:T(128)} %bitcast.2.core_ref, f32[128,128]{1,0:T(8,128)} %copy-done, bf16[32,4096]{1,0:T(8,128)(2,1)} %copy-done.7, bf16[32,4096]{1,0:T(8,128)(2,1)} %copy-done.9, bf16[32,4096]{1,0:T(8,128)(2,1)} %copy-done.10, ...), custom_call_target="tpu_custom_call" | custom-call | flops 268435456 | bytes 4194304 | tf_op jit(solution)/shard_map/pallas_call | solution.py:243
  41.8 1.1 collective-permute-start.11
  42.9 2.6 %collective-permute-done.11 = s32[1]{0:T(128)} collective-permute-done((s32[1]{0:T(128)}, s32[1]{0:T(128)}, u32[]{:S(2)}, u32[]{:S(2)}) %collective-permute-start.11) | collective-permute-done | bytes 36 | tf_op jit(solution)/shard_map/ppermute | solution.py:427
  47.7 1.2 %collective-permute-start.12 = (bf16[128,128]{1,0:T(8,128)(2,1)S(1)}, bf16[128,128]{1,0:T(8,128)(2,1)S(1)}, u32[]{:S(2)}, u32[]{:S(2)}) collective-permute-start(bf16[128,128]{1,0:T(8,128)(2,1)S(1)} %multiply_convert_fusion.coeff_ref), channel_id=1, source_target_pairs={{0,2},{1,3},{2,0},{3,1},{4,6},{5,7},{6,4},{7,5},{8,10},{9,11},{10,... | collective-permute-start | bytes 98312 | tf_op jit(solution)/shard_map/ppermute | solution.py:500
  48.9 4.8 %shard_map.94 = bf16[8,64,1792]{2,1,0:T(8,128)(2,1)} custom-call(bf16[128,256]{1,0:T(8,128)(2,1)S(1)} %get-tuple-element.118.choose_ref, f32[128,128]{1,0:T(8,128)S(1)} %get-tuple-element.119.live_ref, bf16[128,128]{1,0:T(8,128)(2,1)S(1)} %get-tuple-element.120.fixed_ref, bf16[128,128]{1,0:T(8,128)(2,1)S(1)} %multiply_convert_fusion.coeff_ref, ...), custom_call_target="tpu_custom_call" | custom-call | flops 234881024 | bytes 5505024 | tf_op jit(solution)/shard_map/pallas_call | solution.py:286
  53.6 1.6 %collective-permute-start.13 = (bf16[128,128]{1,0:T(8,128)(2,1)S(1)}, bf16[128,128]{1,0:T(8,128)(2,1)S(1)}, u32[]{:S(2)}, u32[]{:S(2)}) collective-permute-start(bf16[128,128]{1,0:T(8,128)(2,1)S(1)} %add.40), channel_id=1, source_target_pairs={{0,4},{1,5},{2,6},{3,7},{4,0},{5,1},{6,2},{7,3},{8,12},{9,13},{10,... | collective-permute-start | bytes 98312 | tf_op jit(solution)/shard_map/ppermute | solution.py:500
  55.3 2.3 %collective-permute-done.13 = bf16[128,128]{1,0:T(8,128)(2,1)S(1)} collective-permute-done((bf16[128,128]{1,0:T(8,128)(2,1)S(1)}, bf16[128,128]{1,0:T(8,128)(2,1)S(1)}, u32[]{:S(2)}, u32[]{:S(2)}) %collective-permute-start.13) | collective-permute-done | bytes 32800 | tf_op jit(solution)/shard_map/ppermute | solution.py:500
  57.6 2.7 %collective-permute-start.14 = (bf16[128,128]{1,0:T(8,128)(2,1)S(1)}, bf16[128,128]{1,0:T(8,128)(2,1)S(1)}, u32[]{:S(2)}, u32[]{:S(2)}) collective-permute-start(bf16[128,128]{1,0:T(8,128)(2,1)S(1)} %add.41), channel_id=1, source_target_pairs={{0,8},{1,9},{2,10},{3,11},{4,12},{5,13},{6,14},{7,15},{8,0},{9,1},... | collective-permute-start | bytes 98312 | tf_op jit(solution)/shard_map/ppermute | solution.py:500
  60.3 2.2 %collective-permute-done.14 = bf16[128,128]{1,0:T(8,128)(2,1)S(1)} collective-permute-done((bf16[128,128]{1,0:T(8,128)(2,1)S(1)}, bf16[128,128]{1,0:T(8,128)(2,1)S(1)}, u32[]{:S(2)}, u32[]{:S(2)}) %collective-permute-start.14) | collective-permute-done | bytes 32800 | tf_op jit(solution)/shard_map/ppermute | solution.py:500
  62.5 5.1 %all-to-all-start.3 = ((bf16[8,64,1792]{2,1,0:T(8,128)(2,1)}), bf16[8,64,1792]{2,1,0:T(8,128)(2,1)S(1)}, u32[]{:S(2)}, u32[]{:S(2)}) async-start(bf16[8,64,1792]{2,1,0:T(8,128)(2,1)} %shard_map.94), calls=%async_computation.3 | async-start | bytes 3670016 | tf_op jit(solution)/shard_map/all_to_all | solution.py:487
  67.7 2.5 %broadcast_select_fusion.1 = (bf16[256,4096]{1,0:T(8,128)(2,1)S(1)}, bf16[256,4096]{1,0:T(8,128)(2,1)S(1)}) fusion(bf16[256,4096]{1,0:T(8,128)(2,1)} %get-tuple-element.126, bf16[256,4096]{1,0:T(8,128)(2,1)} %collective-permute-done.15, pred[]{:T(512)S(6)} %eq.6, pred[]{:T(512)S(6)} %eq.7), kind=kLoop, calls=%fused_computation.5 | loop fusion | flops 2097152 | bytes 8388610 | tf_op jit(solution)/shard_map/jit(_where)/select_n | solution.py:506
  70.2 14.7 %fusion.base_ref = f32[256,1792]{1,0:T(8,128)} fusion(bf16[8192,1792]{1,0:T(8,128)(2,1)} %param.14, bf16[256,4096]{1,0:T(8,128)(2,1)S(1)} %get-tuple-element.135, bf16[256,4096]{1,0:T(8,128)(2,1)S(1)} %get-tuple-element.134), kind=kOutput, calls=%fused_computation | convolution fusion | flops 7524581376 | bytes 35389440 | tf_op jit(solution)/shard_map/dot_general | solution.py:507
  84.9 23.7 %all-to-all-done.3.incoming_ref = bf16[8,64,1792]{2,1,0:T(8,128)(2,1)S(1)} async-done(((bf16[8,64,1792]{2,1,0:T(8,128)(2,1)}), bf16[8,64,1792]{2,1,0:T(8,128)(2,1)S(1)}, u32[]{:S(2)}, u32[]{:S(2)}) %all-to-all-start.3) | async-done | bytes 1835040 | tf_op jit(solution)/shard_map/all_to_all | solution.py:487
  108.5 1.4 %conditional.1 = (bf16[8,64,1792]{2,1,0:T(8,128)(2,1)}) conditional(s32[]{:T(128)} %bitcast.5, () %tuple.31, (bf16[128,256]{1,0:T(8,128)(2,1)S(1)}, f32[128,128]{1,0:T(8,128)S(1)}, bf16[128,128]{1,0:T(8,128)(2,1)S(1)}, bf16[128,128]{1,0:T(8,128)(2,1)S(1)}, bf16[8,64,1792]{2,1,0:T(8,128)(2,1)}, ...), branch_computations={%region_0.1_spmd, %region_1.2_spmd, %region_2.3_spmd, %region_3.4_... | conditional | flops 234881024 | bytes 9175050 | solution.py:525
  108.6 1.4 %broadcast.2 = bf16[8,64,1792]{2,1,0:T(8,128)(2,1)} broadcast(bf16[]{:T(256)} %constant.12.clone), dimensions={} | broadcast | bytes 1835010 | tf_op jit(solution)/shard_map/broadcast.1
  109.9 1.5 %copy-done.5 = f32[256,1792]{1,0:T(8,128)S(1)} copy-done((f32[256,1792]{1,0:T(8,128)S(1)}, f32[256,1792]{1,0:T(8,128)}, u32[]{:S(2)}) %copy-start.5) | copy-done | bytes 1835032
  111.4 4.2 %shard_map.95 = bf16[256,1792]{1,0:T(8,128)(2,1)} custom-call(s32[16]{0:T(128)S(1)} %get-tuple-element.99.begin_ref, s32[1]{0:T(128)S(6)} %max.3.more_ref, f32[256,1792]{1,0:T(8,128)S(1)} %copy-done.5, s32[256,128]{1,0:T(8,128)S(1)} %get-tuple-element.131.code_ref, bf16[128,128]{1,0:T(8,128)(2,1)S(1)} %add.42.coeff_ref, ...), custom_call_target="tpu_custom_call" | custom-call | flops 1879048192 | bytes 6422528 | tf_op jit(solution)/shard_map/pallas_call | solution.py:378
  (42 shorter events, 3.1 us)
Async XLA Ops:
  1.0 4.3 %collective-permute-start = (bf16[16,4096]{1,0:T(8,128)(2,1)S(1)}, bf16[16,4096]{1,0:T(8,128)(2,1)S(1)}, u32[]{:S(2)}, u32[]{:S(2)}) collective-permute-start(bf16[16,4096]{1,0:T(8,128)(2,1)S(1)} %get-tuple-element.137), channel_id=1, source_target_pairs={{0,1},{1,0},{2,3},{3,2},{4,5},{5,4},{6,7},{7,6},{8,9},{9,8},{10,11... | collective-permute-start | bytes 393224 | tf_op jit(solution)/shard_map/ppermute | solution.py:457
  1.5 7.0 %copy-start.1 = (s32[16]{0:T(128)S(1)}, s32[16]{0:T(128)}, u32[]{:S(2)}) copy-start(s32[16]{0:T(128)} %ranks_in.1) | copy-start | bytes 196
  1.5 7.0 %copy-start.2 = (s32[16]{0:T(128)S(1)}, s32[16]{0:T(128)}, u32[]{:S(2)}) copy-start(s32[16]{0:T(128)} %home_in.1) | copy-start | bytes 196
  1.5 7.0 %copy-start.3 = (s32[16]{0:T(128)S(1)}, s32[16]{0:T(128)}, u32[]{:S(2)}) copy-start(s32[16]{0:T(128)} %length_in.1) | copy-start | bytes 196
  1.5 7.0 %copy-start.4 = (s32[16]{0:T(128)S(1)}, s32[16]{0:T(128)}, u32[]{:S(2)}) copy-start(s32[16]{0:T(128)} %adapter_in.1) | copy-start | bytes 196
  5.3 57.3 %copy-start.6 = (bf16[8,64,1792]{2,1,0:T(8,128)(2,1)}, bf16[8,64,1792]{2,1,0:T(8,128)(2,1)S(1)}, u32[]{:S(2)}) copy-start(bf16[8,64,1792]{2,1,0:T(8,128)(2,1)S(1)} %get-tuple-element.121.mine_ref) | copy-start | bytes 5505028
  5.3 31.1 %copy-start.7 = (bf16[32,4096]{1,0:T(8,128)(2,1)}, bf16[32,4096]{1,0:T(8,128)(2,1)S(1)}, u32[]{:S(2)}) copy-start(bf16[32,4096]{1,0:T(8,128)(2,1)S(1)} %pad_maximum_fusion.refs_0_) | copy-start | bytes 786436
  5.3 17.4 %collective-permute-start.4 = (bf16[8,64,1792]{2,1,0:T(8,128)(2,1)}, bf16[8,64,1792]{2,1,0:T(8,128)(2,1)}, u32[]{:S(2)}, u32[]{:S(2)}) collective-permute-start(bf16[8,64,1792]{2,1,0:T(8,128)(2,1)} %get-tuple-element.108), channel_id=1, source_target_pairs={{0,1},{1,0},{2,3},{3,2},{4,5},{5,4},{6,7},{7,6},{8,9},{9,8},{10,11... | collective-permute-start | bytes 5505032 | tf_op jit(solution)/shard_map/ppermute | solution.py:462
  5.4 9.5 %collective-permute-start.1 = (bf16[32,4096]{1,0:T(8,128)(2,1)S(1)}, bf16[32,4096]{1,0:T(8,128)(2,1)S(1)}, u32[]{:S(2)}, u32[]{:S(2)}) collective-permute-start(bf16[32,4096]{1,0:T(8,128)(2,1)S(1)} %pad_maximum_fusion.refs_0_), channel_id=1, source_target_pairs={{0,4},{1,5},{4,8},{5,9},{8,12},{9,13},{12,14},{13,15},{14,10},{15,... | collective-permute-start | bytes 786440 | tf_op jit(solution)/shard_map/ppermute | solution.py:411
  8.5 14.2 %collective-permute-start.5 = (bf16[64,4096]{1,0:T(8,128)(2,1)}, bf16[64,4096]{1,0:T(8,128)(2,1)S(1)}, u32[]{:S(2)}, u32[]{:S(2)}) collective-permute-start(bf16[64,4096]{1,0:T(8,128)(2,1)} %get-tuple-element.109), channel_id=1, source_target_pairs={{0,1},{1,0},{2,3},{3,2},{4,5},{5,4},{6,7},{7,6},{8,9},{9,8},{10,11... | collective-permute-start | bytes 1572872 | tf_op jit(solution)/shard_map/ppermute | solution.py:463
  10.6 0.6 copy-start
  11.2 8.7 %collective-permute-start.2 = (bf16[32,4096]{1,0:T(8,128)(2,1)S(1)}, bf16[32,4096]{1,0:T(8,128)(2,1)S(1)}, u32[]{:S(2)}, u32[]{:S(2)}) collective-permute-start(bf16[32,4096]{1,0:T(8,128)(2,1)S(1)} %pad_maximum_fusion.refs_0_), channel_id=1, source_target_pairs={{4,0},{5,1},{8,4},{9,5},{12,8},{13,9},{14,12},{15,13},{10,14},{11,... | collective-permute-start | bytes 786440 | tf_op jit(solution)/shard_map/ppermute | solution.py:413
  14.9 21.5 %copy-start.9 = (bf16[32,4096]{1,0:T(8,128)(2,1)}, bf16[32,4096]{1,0:T(8,128)(2,1)S(1)}, u32[]{:S(2)}) copy-start(bf16[32,4096]{1,0:T(8,128)(2,1)S(1)} %collective-permute-done.1.refs_1_) | copy-start | bytes 786436
  14.9 7.8 %collective-permute-start.3 = (bf16[32,4096]{1,0:T(8,128)(2,1)S(1)}, bf16[32,4096]{1,0:T(8,128)(2,1)S(1)}, u32[]{:S(2)}, u32[]{:S(2)}) collective-permute-start(bf16[32,4096]{1,0:T(8,128)(2,1)S(1)} %collective-permute-done.1.refs_1_), channel_id=1, source_target_pairs={{0,4},{1,5},{4,8},{5,9},{8,12},{9,13},{12,14},{13,15},{14,10},{15,... | collective-permute-start | bytes 786440 | tf_op jit(solution)/shard_map/ppermute | solution.py:411
  19.9 16.5 %copy-start.10 = (bf16[32,4096]{1,0:T(8,128)(2,1)}, bf16[32,4096]{1,0:T(8,128)(2,1)S(1)}, u32[]{:S(2)}) copy-start(bf16[32,4096]{1,0:T(8,128)(2,1)S(1)} %collective-permute-done.2.refs_2_) | copy-start | bytes 786436
  19.9 8.0 %collective-permute-start.6 = (bf16[32,4096]{1,0:T(8,128)(2,1)S(1)}, bf16[32,4096]{1,0:T(8,128)(2,1)}, u32[]{:S(2)}, u32[]{:S(2)}) collective-permute-start(bf16[32,4096]{1,0:T(8,128)(2,1)S(1)} %collective-permute-done.2.refs_2_), channel_id=1, source_target_pairs={{4,0},{5,1},{8,4},{9,5},{12,8},{13,9},{14,12},{15,13},{10,14},{11,... | collective-permute-start | bytes 786440 | tf_op jit(solution)/shard_map/ppermute | solution.py:413
  22.7 5.3 %copy-start.11 = (bf16[32,4096]{1,0:T(8,128)(2,1)}, bf16[32,4096]{1,0:T(8,128)(2,1)S(1)}, u32[]{:S(2)}) copy-start(bf16[32,4096]{1,0:T(8,128)(2,1)S(1)} %collective-permute-done.3.refs_3_) | copy-start | bytes 786436
  22.7 13.7 %copy-start.8 = (bf16[64,4096]{1,0:T(8,128)(2,1)}, bf16[64,4096]{1,0:T(8,128)(2,1)S(1)}, u32[]{:S(2)}) copy-start(bf16[64,4096]{1,0:T(8,128)(2,1)S(1)} %collective-permute-done.5.refs_9_) | copy-start | bytes 1572868
  22.7 7.0 %collective-permute-start.7 = (bf16[32,4096]{1,0:T(8,128)(2,1)S(1)}, bf16[32,4096]{1,0:T(8,128)(2,1)}, u32[]{:S(2)}, u32[]{:S(2)}) collective-permute-start(bf16[32,4096]{1,0:T(8,128)(2,1)S(1)} %collective-permute-done.3.refs_3_), channel_id=1, source_target_pairs={{0,4},{1,5},{4,8},{5,9},{8,12},{9,13},{12,14},{13,15},{14,10},{15,... | collective-permute-start | bytes 786440 | tf_op jit(solution)/shard_map/ppermute | solution.py:411
  28.0 7.3 %collective-permute-start.8 = (bf16[32,4096]{1,0:T(8,128)(2,1)}, bf16[32,4096]{1,0:T(8,128)(2,1)}, u32[]{:S(2)}, u32[]{:S(2)}) collective-permute-start(bf16[32,4096]{1,0:T(8,128)(2,1)} %collective-permute-done.6.refs_4_), channel_id=1, source_target_pairs={{4,0},{5,1},{8,4},{9,5},{12,8},{13,9},{14,12},{15,13},{10,14},{11,... | collective-permute-start | bytes 786440 | tf_op jit(solution)/shard_map/ppermute | solution.py:413
  29.7 6.7 %collective-permute-start.9 = (bf16[32,4096]{1,0:T(8,128)(2,1)}, bf16[32,4096]{1,0:T(8,128)(2,1)}, u32[]{:S(2)}, u32[]{:S(2)}) collective-permute-start(bf16[32,4096]{1,0:T(8,128)(2,1)} %collective-permute-done.7.refs_5_), channel_id=1, source_target_pairs={{0,4},{1,5},{4,8},{5,9},{8,12},{9,13},{12,14},{13,15},{14,10},{15,... | collective-permute-start | bytes 786440 | tf_op jit(solution)/shard_map/ppermute | solution.py:411
  41.7 5.0 %collective-permute-start.10 = (f32[128,128]{1,0:T(8,128)}, f32[128,128]{1,0:T(8,128)S(1)}, u32[]{:S(2)}, u32[]{:S(2)}) collective-permute-start(f32[128,128]{1,0:T(8,128)} %get-tuple-element.112), channel_id=1, source_target_pairs={{0,1},{1,0},{2,3},{3,2},{4,5},{5,4},{6,7},{7,6},{8,9},{9,8},{10,11... | collective-permute-start | bytes 196616 | tf_op jit(solution)/shard_map/ppermute | solution.py:479
  41.8 3.8 %collective-permute-start.11 = (s32[1]{0:T(128)}, s32[1]{0:T(128)}, u32[]{:S(2)}, u32[]{:S(2)}) collective-permute-start(s32[1]{0:T(128)} %get-tuple-element.115), channel_id=1, source_target_pairs={{0,16},{16,0},{1,17},{17,1},{2,18},{18,2},{3,19},{19,3},{4,20},{20... | collective-permute-start | bytes 20 | tf_op jit(solution)/shard_map/ppermute | solution.py:427
  47.6 14.9 %collective-permute-start.15 = (bf16[256,4096]{1,0:T(8,128)(2,1)}, bf16[256,4096]{1,0:T(8,128)(2,1)}, u32[]{:S(2)}, u32[]{:S(2)}) collective-permute-start(bf16[256,4096]{1,0:T(8,128)(2,1)} %get-tuple-element.126), channel_id=1, source_target_pairs={{0,1},{1,0},{2,3},{3,2},{4,5},{5,4},{6,7},{7,6},{8,9},{9,8},{10,11... | collective-permute-start | bytes 6291464 | tf_op jit(solution)/shard_map/ppermute | solution.py:497
  47.7 5.9 %collective-permute-start.12 = (bf16[128,128]{1,0:T(8,128)(2,1)S(1)}, bf16[128,128]{1,0:T(8,128)(2,1)S(1)}, u32[]{:S(2)}, u32[]{:S(2)}) collective-permute-start(bf16[128,128]{1,0:T(8,128)(2,1)S(1)} %multiply_convert_fusion.coeff_ref), channel_id=1, source_target_pairs={{0,2},{1,3},{2,0},{3,1},{4,6},{5,7},{6,4},{7,5},{8,10},{9,11},{10,... | collective-permute-start | bytes 98312 | tf_op jit(solution)/shard_map/ppermute | solution.py:500
  53.6 4.0 %collective-permute-start.13 = (bf16[128,128]{1,0:T(8,128)(2,1)S(1)}, bf16[128,128]{1,0:T(8,128)(2,1)S(1)}, u32[]{:S(2)}, u32[]{:S(2)}) collective-permute-start(bf16[128,128]{1,0:T(8,128)(2,1)S(1)} %add.40), channel_id=1, source_target_pairs={{0,4},{1,5},{2,6},{3,7},{4,0},{5,1},{6,2},{7,3},{8,12},{9,13},{10,... | collective-permute-start | bytes 98312 | tf_op jit(solution)/shard_map/ppermute | solution.py:500
  57.6 4.9 %collective-permute-start.14 = (bf16[128,128]{1,0:T(8,128)(2,1)S(1)}, bf16[128,128]{1,0:T(8,128)(2,1)S(1)}, u32[]{:S(2)}, u32[]{:S(2)}) collective-permute-start(bf16[128,128]{1,0:T(8,128)(2,1)S(1)} %add.41), channel_id=1, source_target_pairs={{0,8},{1,9},{2,10},{3,11},{4,12},{5,13},{6,14},{7,15},{8,0},{9,1},... | collective-permute-start | bytes 98312 | tf_op jit(solution)/shard_map/ppermute | solution.py:500
  62.5 46.0 %all-to-all-start.3 = ((bf16[8,64,1792]{2,1,0:T(8,128)(2,1)}), bf16[8,64,1792]{2,1,0:T(8,128)(2,1)S(1)}, u32[]{:S(2)}, u32[]{:S(2)}) async-start(bf16[8,64,1792]{2,1,0:T(8,128)(2,1)} %shard_map.94), calls=%async_computation.3 | async-start | bytes 3670016 | tf_op jit(solution)/shard_map/all_to_all | solution.py:487
  109.9 1.5 %copy-start.5 = (f32[256,1792]{1,0:T(8,128)S(1)}, f32[256,1792]{1,0:T(8,128)}, u32[]{:S(2)}) copy-start(f32[256,1792]{1,0:T(8,128)} %fusion.base_ref) | copy-start | bytes 5505028
where the time goes:
time: 116 us
  waiting for transfers between devices  49.6 us (43%)
  starting transfers between devices  20.8 us (18%)
  Pallas kernels  20 us (17%)
  matrix products  14.7 us (13%)
  local copies, waits for them, and re-layouts  5.71 us (5%)
  other arithmetic  3.41 us (3%)
  between operations  1.36 us (1%)
    all_to_all x1, waiting for transfers between devices, exchange(): lax.all_to_all(value, 'tensor', split_axis=0, concat_axis=0, axis_index_g...  23.7 us
    dot_general x1, matrix products, pooled(): jnp.dot(jnp.concatenate(halves, axis=1), up_weight, preferred_element_typ...  14.7 us
    ppermute x3, waiting for transfers between devices, ring_gather(): held[step] = lax.ppermute(held[step - 1], 'tensor', back)  10.1 us
    ppermute x4, waiting for transfers between devices, ring_gather(): held[-step] = lax.ppermute(held[1 - step], 'tensor', ahead)  8.59 us
    ppermute x4, starting transfers between devices, ring_gather(): held[-step] = lax.ppermute(held[1 - step], 'tensor', ahead)  7.5 us
    ppermute x3, starting transfers between devices, pooled(): lax.ppermute(every, 'tensor', [(t, t ^ bit) for t in range(shards)])  5.46 us
    pallas_call x1, Pallas kernels, collect_rows(): pl.pallas_call(kernel, in_specs=[smem, smem, whole] + [pl.BlockSpec(memor...  5.27 us
    all_to_all x1, starting transfers between devices, exchange(): lax.all_to_all(value, 'tensor', split_axis=0, concat_axis=0, axis_index_g...  5.13 us
  transfers between devices with their start and end apart: 17, of which 11 were waited for; matrix products, arithmetic and copies ran while one was open for 16% of the time, Pallas kernels for 9%

commit v1 on v0

--- a/solution.py
+++ b/solution.py
@@ -389,7 +389,7 @@
             pltpu.VMEM(incoming.shape, incoming.dtype),
             pltpu.SemaphoreType.DMA((3,)),
         ],
-        compiler_params=vmem(8 * total_rows * width + 2 * chips * limit * width),
+        compiler_params=pltpu.CompilerParams(vmem_limit_bytes=WIDE_GRANT),
         cost_estimate=pl.CostEstimate(
             flops=4 * total_rows * chips * limit * width,
             bytes_accessed=6 * total_rows * width + 2 * chips * limit * width,
@@ -507,14 +507,16 @@
     base = jnp.dot(
         jnp.concatenate(halves, axis=1), up_weight, preferred_element_type=jnp.float32
     )
-    fullest, base, incoming = lax.optimization_barrier((fullest, base, incoming))
+    choose, base = lax.optimization_barrier((choose, base))
     rest = limit - FIRST_ROWS
+    far = payload(FIRST_ROWS, rest)
+    fullest, base, incoming, far = lax.optimization_barrier((fullest, base, incoming, far))
 
     def later(count):
         def run():
             value = jnp.zeros((chips, rest - count, up_weight.shape[1]), adapter_up.dtype)
             if count:
-                late = exchange(payload(FIRST_ROWS, count))
+                late = exchange(far[:, :count])
                 value = jnp.concatenate([late, value], axis=1)
             return value
 

time: 116 us -> 145 us (1.25)
  blocking collectives: 0 us -> 26.7 us
  Pallas kernels: 20 us -> 25.1 us
  waiting for transfers between devices: 49.6 us -> 45.3 us
    all_to_all x0 -> x1, blocking collectives: none -> 26.7 us  [exchange(): lax.all_to_all(value, 'tensor', split_axis=0, concat_axis=0, axis_index_g...]
    all_to_all x1, waiting for transfers between devices: 23.7 us -> 20.3 us  [exchange(): lax.all_to_all(value, 'tensor', split_axis=0, concat_axis=0, axis_index_g...]
    pallas_call x1, Pallas kernels: 4.15 us -> 6.92 us  [combine(): pl.pallas_call(kernel, in_specs=[smem] * 2 + [pl.BlockSpec(memory_space=p...]
    pallas_call x1 -> x2, Pallas kernels: 4.76 us -> 6.5 us  [build_payload(): pl.pallas_call(kernel, in_specs=[pl.BlockSpec(memory_space=pltpu.VMEM)] *...]
  transfers between devices with their start and end apart: 17 -> 17, of which waited for: 11 -> 11; matrix products, arithmetic and copies ran while one was open for 16% -> 13% of each run, Pallas kernels for 9% -> 9%
where the time goes in v1:
time: 145 us; the launch traced here: 144 us
  waiting for transfers between devices  45.3 us (31%)
  blocking collectives  26.7 us (18%)
  Pallas kernels  25.1 us (17%)
  starting transfers between devices  20.8 us (14%)
  matrix products  14.8 us (10%)
  local copies, waits for them, and re-layouts  6.23 us (4%)
  other arithmetic  4.01 us (3%)
  between operations  1.5 us (1%)
    all_to_all x1, blocking collectives, exchange(): lax.all_to_all(value, 'tensor', split_axis=0, concat_axis=0, axis_index_g...  26.7 us
    all_to_all x1, waiting for transfers between devices, exchange(): lax.all_to_all(value, 'tensor', split_axis=0, concat_axis=0, axis_index_g...  20.3 us
    dot_general x1, matrix products, pooled(): jnp.dot(jnp.concatenate(halves, axis=1), up_weight, preferred_element_typ...  14.8 us
    ppermute x3, waiting for transfers between devices, ring_gather(): held[step] = lax.ppermute(held[step - 1], 'tensor', back)  9.43 us
    ppermute x4, waiting for transfers between devices, ring_gather(): held[-step] = lax.ppermute(held[1 - step], 'tensor', ahead)  8.51 us
    ppermute x4, starting transfers between devices, ring_gather(): held[-step] = lax.ppermute(held[1 - step], 'tensor', ahead)  7.43 us
    pallas_call x1, Pallas kernels, combine(): pl.pallas_call(kernel, in_specs=[smem] * 2 + [pl.BlockSpec(memory_space=p...  6.92 us
    pallas_call x2, Pallas kernels, build_payload(): pl.pallas_call(kernel, in_specs=[pl.BlockSpec(memory_space=pltpu.VMEM)] *...  6.5 us
  transfers between devices with their start and end apart: 17, of which 11 were waited for; matrix products, arithmetic and copies ran while one was open for 13% of the time, Pallas kernels for 9%

profile of v1, /device:TPU:0, one launch (start us, length us, event | category | flops | bytes accessed | tf_op | source)
XLA Modules:
  0.0 144.4 jit_solution(444346206021824637)
XLA Ops:
  1.5 4.3 %shard_map.92 = (bf16[8,64,1792]{2,1,0:T(8,128)(2,1)}, bf16[8,64,1792]{2,1,0:T(8,128)(2,1)}, bf16[64,4096]{1,0:T(8,128)(2,1)}) custom-call(s32[1]{0:T(128)} %bitcast.2.core_ref, bf16[64,28672]{1,0:T(8,128)(2,1)} %bitcast.10, bf16[64,8192]{1,0:T(8,128)(2,1)} %bitcast.8), custom_call_target="tpu_custom_call" | custom-call | bytes 7340032 | tf_op jit(solution)/shard_map/pallas_call | solution.py:63
  6.0 3.0 %collective-permute-start.1 = (bf16[32,4096]{1,0:T(8,128)(2,1)S(1)}, bf16[32,4096]{1,0:T(8,128)(2,1)S(1)}, u32[]{:S(2)}, u32[]{:S(2)}) collective-permute-start(bf16[32,4096]{1,0:T(8,128)(2,1)S(1)} %pad_maximum_fusion.refs_0_), channel_id=1, source_target_pairs={{0,4},{1,5},{4,8},{5,9},{8,12},{9,13},{12,14},{13,15},{14,10},{15,... | collective-permute-start | bytes 786440 | tf_op jit(solution)/shard_map/ppermute | solution.py:411
  9.1 2.1 %shard_map.91 = (f32[128,128]{1,0:T(8,128)S(1)}, f32[128,128]{1,0:T(8,128)S(1)}, bf16[128,256]{1,0:T(8,128)(2,1)S(1)}, f32[128,128]{1,0:T(8,128)S(1)}, bf16[128,...) custom-call(s32[16]{0:T(128)S(1)} %copy-done.5, s32[16]{0:T(128)S(1)} %copy-done.6, ...), custom_call_target="tpu_custom_call" | custom-call | flops 6553600 | bytes 524288 | tf_op jit(solution)/shard_map/pallas_call | solution.py:159
  12.6 3.0 %collective-permute-done.1.refs_1_ = bf16[32,4096]{1,0:T(8,128)(2,1)S(1)} collective-permute-done((bf16[32,4096]{1,0:T(8,128)(2,1)S(1)}, bf16[32,4096]{1,0:T(8,128)(2,1)S(1)}, u32[]{:S(2)}, u32[]{:S(2)}) %collective-permute-start.1) | collective-permute-done | bytes 262176 | tf_op jit(solution)/shard_map/ppermute | solution.py:411
  15.6 1.8 %collective-permute-start.3 = (bf16[32,4096]{1,0:T(8,128)(2,1)S(1)}, bf16[32,4096]{1,0:T(8,128)(2,1)S(1)}, u32[]{:S(2)}, u32[]{:S(2)}) collective-permute-start(bf16[32,4096]{1,0:T(8,128)(2,1)S(1)} %collective-permute-done.1.refs_1_), channel_id=1, source_target_pairs={{0,4},{1,5},{4,8},{5,9},{8,12},{9,13},{12,14},{13,15},{14,10},{15,... | collective-permute-start | bytes 786440 | tf_op jit(solution)/shard_map/ppermute | solution.py:411
  17.3 3.8 %collective-permute-done.2.refs_2_ = bf16[32,4096]{1,0:T(8,128)(2,1)S(1)} collective-permute-done((bf16[32,4096]{1,0:T(8,128)(2,1)S(1)}, bf16[32,4096]{1,0:T(8,128)(2,1)S(1)}, u32[]{:S(2)}, u32[]{:S(2)}) %collective-permute-start.2) | collective-permute-done | bytes 262176 | tf_op jit(solution)/shard_map/ppermute | solution.py:413
  21.5 1.8 %collective-permute-done.3.refs_3_ = bf16[32,4096]{1,0:T(8,128)(2,1)S(1)} collective-permute-done((bf16[32,4096]{1,0:T(8,128)(2,1)S(1)}, bf16[32,4096]{1,0:T(8,128)(2,1)S(1)}, u32[]{:S(2)}, u32[]{:S(2)}) %collective-permute-start.3) | collective-permute-done | bytes 262176 | tf_op jit(solution)/shard_map/ppermute | solution.py:411
  23.3 1.3 copy-done.1
  24.6 1.5 %collective-permute-start.7 = (bf16[32,4096]{1,0:T(8,128)(2,1)S(1)}, bf16[32,4096]{1,0:T(8,128)(2,1)}, u32[]{:S(2)}, u32[]{:S(2)}) collective-permute-start(bf16[32,4096]{1,0:T(8,128)(2,1)S(1)} %collective-permute-done.3.refs_3_), channel_id=1, source_target_pairs={{0,4},{1,5},{4,8},{5,9},{8,12},{9,13},{12,14},{13,15},{14,10},{15,... | collective-permute-start | bytes 786440 | tf_op jit(solution)/shard_map/ppermute | solution.py:411
  26.1 3.1 %collective-permute-done.6.refs_4_ = bf16[32,4096]{1,0:T(8,128)(2,1)} collective-permute-done((bf16[32,4096]{1,0:T(8,128)(2,1)S(1)}, bf16[32,4096]{1,0:T(8,128)(2,1)}, u32[]{:S(2)}, u32[]{:S(2)}) %collective-permute-start.6) | collective-permute-done | bytes 262176 | tf_op jit(solution)/shard_map/ppermute | solution.py:413
  29.6 2.0 %collective-permute-done.7.refs_5_ = bf16[32,4096]{1,0:T(8,128)(2,1)} collective-permute-done((bf16[32,4096]{1,0:T(8,128)(2,1)S(1)}, bf16[32,4096]{1,0:T(8,128)(2,1)}, u32[]{:S(2)}, u32[]{:S(2)}) %collective-permute-start.7) | collective-permute-done | bytes 262176 | tf_op jit(solution)/shard_map/ppermute | solution.py:411
  31.6 1.1 collective-permute-start.9
  32.7 1.3 fusion.4.places_ref
  34.1 2.5 %collective-permute-done.8.refs_6_ = bf16[32,4096]{1,0:T(8,128)(2,1)} collective-permute-done((bf16[32,4096]{1,0:T(8,128)(2,1)}, bf16[32,4096]{1,0:T(8,128)(2,1)}, u32[]{:S(2)}, u32[]{:S(2)}) %collective-permute-start.8) | collective-permute-done | bytes 262176 | tf_op jit(solution)/shard_map/ppermute | solution.py:413
  36.6 1.7 %collective-permute-done.9.refs_7_ = bf16[32,4096]{1,0:T(8,128)(2,1)} collective-permute-done((bf16[32,4096]{1,0:T(8,128)(2,1)}, bf16[32,4096]{1,0:T(8,128)(2,1)}, u32[]{:S(2)}, u32[]{:S(2)}) %collective-permute-start.9) | collective-permute-done | bytes 262176 | tf_op jit(solution)/shard_map/ppermute | solution.py:411
  38.3 5.3 %shard_map.93 = (bf16[256,4096]{1,0:T(8,128)(2,1)}, f32[128,128]{1,0:T(8,128)}) custom-call(s32[16]{0:T(128)} %fusion.4.places_ref, s32[1]{0:T(128)} %bitcast.2.core_ref, f32[128,128]{1,0:T(8,128)} %copy-done.4, bf16[32,4096]{1,0:T(8,128)(2,1)} %copy-done.11, bf16[32,4096]{1,0:T(8,128)(2,1)} %copy-done.13, bf16[32,4096]{1,0:T(8,128)(2,1)} %copy-done.14, ...), custom_call_target="tpu_custom_call" | custom-call | flops 268435456 | bytes 4194304 | tf_op jit(solution)/shard_map/pallas_call | solution.py:243
  44.7 2.5 %collective-permute-done.11 = s32[1]{0:T(128)} collective-permute-done((s32[1]{0:T(128)}, s32[1]{0:T(128)}, u32[]{:S(2)}, u32[]{:S(2)}) %collective-permute-start.11) | collective-permute-done | bytes 36 | tf_op jit(solution)/shard_map/ppermute | solution.py:427
  49.5 1.1 collective-permute-start.12
  50.6 3.2 %shard_map.94 = bf16[8,64,1792]{2,1,0:T(8,128)(2,1)} custom-call(bf16[128,256]{1,0:T(8,128)(2,1)S(1)} %get-tuple-element.82.choose_ref, f32[128,128]{1,0:T(8,128)S(1)} %get-tuple-element.71.live_ref, bf16[128,128]{1,0:T(8,128)(2,1)S(1)} %get-tuple-element.72.fixed_ref, bf16[128,128]{1,0:T(8,128)(2,1)S(1)} %multiply_convert_fusion.coeff_ref, ...), custom_call_target="tpu_custom_call" | custom-call | flops 234881024 | bytes 5505024 | tf_op jit(solution)/shard_map/pallas_call | solution.py:286
  53.9 1.6 %collective-permute-start.13 = (bf16[128,128]{1,0:T(8,128)(2,1)S(1)}, bf16[128,128]{1,0:T(8,128)(2,1)S(1)}, u32[]{:S(2)}, u32[]{:S(2)}) collective-permute-start(bf16[128,128]{1,0:T(8,128)(2,1)S(1)} %add.40), channel_id=1, source_target_pairs={{0,4},{1,5},{2,6},{3,7},{4,0},{5,1},{6,2},{7,3},{8,12},{9,13},{10,... | collective-permute-start | bytes 98312 | tf_op jit(solution)/shard_map/ppermute | solution.py:500
  55.5 2.3 %collective-permute-done.13 = bf16[128,128]{1,0:T(8,128)(2,1)S(1)} collective-permute-done((bf16[128,128]{1,0:T(8,128)(2,1)S(1)}, bf16[128,128]{1,0:T(8,128)(2,1)S(1)}, u32[]{:S(2)}, u32[]{:S(2)}) %collective-permute-start.13) | collective-permute-done | bytes 32800 | tf_op jit(solution)/shard_map/ppermute | solution.py:500
  57.9 2.7 %collective-permute-start.14 = (bf16[128,128]{1,0:T(8,128)(2,1)S(1)}, bf16[128,128]{1,0:T(8,128)(2,1)S(1)}, u32[]{:S(2)}, u32[]{:S(2)}) collective-permute-start(bf16[128,128]{1,0:T(8,128)(2,1)S(1)} %add.41), channel_id=1, source_target_pairs={{0,8},{1,9},{2,10},{3,11},{4,12},{5,13},{6,14},{7,15},{8,0},{9,1},... | collective-permute-start | bytes 98312 | tf_op jit(solution)/shard_map/ppermute | solution.py:500
  60.6 2.2 %collective-permute-done.14 = bf16[128,128]{1,0:T(8,128)(2,1)S(1)} collective-permute-done((bf16[128,128]{1,0:T(8,128)(2,1)S(1)}, bf16[128,128]{1,0:T(8,128)(2,1)S(1)}, u32[]{:S(2)}, u32[]{:S(2)}) %collective-permute-start.14) | collective-permute-done | bytes 32800 | tf_op jit(solution)/shard_map/ppermute | solution.py:500
  63.4 5.2 %all-to-all-start.3 = ((bf16[8,64,1792]{2,1,0:T(8,128)(2,1)}), bf16[8,64,1792]{2,1,0:T(8,128)(2,1)}, u32[]{:S(2)}, u32[]{:S(2)}) async-start(bf16[8,64,1792]{2,1,0:T(8,128)(2,1)} %shard_map.94), calls=%async_computation.3 | async-start | bytes 3670016 | tf_op jit(solution)/shard_map/all_to_all | solution.py:487
  68.6 2.5 %broadcast_select_fusion.1 = (bf16[256,4096]{1,0:T(8,128)(2,1)S(1)}, bf16[256,4096]{1,0:T(8,128)(2,1)S(1)}) fusion(bf16[256,4096]{1,0:T(8,128)(2,1)} %get-tuple-element.78, bf16[256,4096]{1,0:T(8,128)(2,1)} %collective-permute-done.15, pred[]{:T(512)S(6)} %eq.6, pred[]{:T(512)S(6)} %eq.7), kind=kLoop, calls=%fused_computation.5 | loop fusion | flops 2097152 | bytes 8388610 | tf_op jit(solution)/shard_map/jit(_where)/select_n | solution.py:506
  71.1 14.8 %fusion.base_ref = f32[256,1792]{1,0:T(8,128)} fusion(bf16[8192,1792]{1,0:T(8,128)(2,1)} %param.14, bf16[256,4096]{1,0:T(8,128)(2,1)S(1)} %get-tuple-element.90, bf16[256,4096]{1,0:T(8,128)(2,1)S(1)} %get-tuple-element.89), kind=kOutput, calls=%fused_computation | convolution fusion | flops 7524581376 | bytes 35389440 | tf_op jit(solution)/shard_map/dot_general | solution.py:507
  86.0 3.3 %shard_map.95 = bf16[8,64,1792]{2,1,0:T(8,128)(2,1)} custom-call(bf16[128,256]{1,0:T(8,128)(2,1)S(1)} %get-tuple-element.82.choose_ref, f32[128,128]{1,0:T(8,128)S(1)} %get-tuple-element.71.live_ref, bf16[128,128]{1,0:T(8,128)(2,1)S(1)} %get-tuple-element.72.fixed_ref, bf16[128,128]{1,0:T(8,128)(2,1)S(1)} %multiply_convert_fusion.coeff_ref, ...), custom_call_target="tpu_custom_call" | custom-call | flops 234881024 | bytes 5505024 | tf_op jit(solution)/shard_map/pallas_call | solution.py:286
  89.2 20.3 %all-to-all-done.3.incoming_ref = bf16[8,64,1792]{2,1,0:T(8,128)(2,1)} async-done(((bf16[8,64,1792]{2,1,0:T(8,128)(2,1)}), bf16[8,64,1792]{2,1,0:T(8,128)(2,1)}, u32[]{:S(2)}, u32[]{:S(2)}) %all-to-all-start.3) | async-done | bytes 1835040 | tf_op jit(solution)/shard_map/all_to_all | solution.py:487
  109.5 28.0 %conditional.1 = (bf16[8,64,1792]{2,1,0:T(8,128)(2,1)S(1)}) conditional(s32[]{:T(128)} %bitcast.5, () %tuple.33, bf16[8,64,1792]{2,1,0:T(8,128)(2,1)} %shard_map.95, bf16[8,64,1792]{2,1,0:T(8,128)(2,1)} %shard_map.95, bf16[8,64,1792]{2,1,0:T(8,128)(2,1)} %shard_map.95), branch_computations={%region_0.1_spmd, %region_1.2_spmd, %region_2.3_spmd, %region_3.4_... | conditional | bytes 7340066 | solution.py:527
  109.5 1.2 slice-done
  110.7 26.7 %all_to_all.18 = bf16[8,32,1792]{2,1,0:T(8,128)(2,1)S(1)} all-to-all(bf16[8,32,1792]{2,1,0:T(8,128)(2,1)S(1)} %slice-done), channel_id=1, replica_groups={{0,2,4,6,8,10,12,14},{1,3,5,7,9,11,13,15},{16,18,20,22,24,26,28,30},{17..., dimensions={0} | all-to-all | bytes 1835008 | tf_op jit(solution)/shard_map/cond/branch_2_fun/all_to_all | solution.py:487
  137.5 6.9 %shard_map.96 = bf16[256,1792]{1,0:T(8,128)(2,1)} custom-call(s32[16]{0:T(128)} %copy-done.10, s32[1]{0:T(128)S(6)} %max.3.more_ref, f32[256,1792]{1,0:T(8,128)} %fusion.base_ref, s32[256,128]{1,0:T(8,128)} %copy-done.9, bf16[128,128]{1,0:T(8,128)(2,1)} %add.42.coeff_ref, bf16[8,64,1792]{2,1,0:T(8,128)(2,1)} %all-to-all-done.3.incoming_ref, ...), custom_call_target="tpu_custom_call" | custom-call | flops 1879048192 | bytes 6422528 | tf_op jit(solution)/shard_map/pallas_call | solution.py:378
  (54 shorter events, 6.6 us)
Async XLA Ops:
  1.0 4.9 %collective-permute-start = (bf16[16,4096]{1,0:T(8,128)(2,1)S(1)}, bf16[16,4096]{1,0:T(8,128)(2,1)S(1)}, u32[]{:S(2)}, u32[]{:S(2)}) collective-permute-start(bf16[16,4096]{1,0:T(8,128)(2,1)S(1)} %get-tuple-element.92), channel_id=1, source_target_pairs={{0,1},{1,0},{2,3},{3,2},{4,5},{5,4},{6,7},{7,6},{8,9},{9,8},{10,11... | collective-permute-start | bytes 393224 | tf_op jit(solution)/shard_map/ppermute | solution.py:457
  1.5 7.6 %copy-start.5 = (s32[16]{0:T(128)S(1)}, s32[16]{0:T(128)}, u32[]{:S(2)}) copy-start(s32[16]{0:T(128)} %ranks_in.1) | copy-start | bytes 196
  1.5 7.6 %copy-start.6 = (s32[16]{0:T(128)S(1)}, s32[16]{0:T(128)}, u32[]{:S(2)}) copy-start(s32[16]{0:T(128)} %home_in.1) | copy-start | bytes 196
  1.5 7.6 %copy-start.7 = (s32[16]{0:T(128)S(1)}, s32[16]{0:T(128)}, u32[]{:S(2)}) copy-start(s32[16]{0:T(128)} %length_in.1) | copy-start | bytes 196
  1.5 7.6 %copy-start.8 = (s32[16]{0:T(128)S(1)}, s32[16]{0:T(128)}, u32[]{:S(2)}) copy-start(s32[16]{0:T(128)} %adapter_in.1) | copy-start | bytes 196
  5.9 32.4 %copy-start.11 = (bf16[32,4096]{1,0:T(8,128)(2,1)}, bf16[32,4096]{1,0:T(8,128)(2,1)S(1)}, u32[]{:S(2)}) copy-start(bf16[32,4096]{1,0:T(8,128)(2,1)S(1)} %pad_maximum_fusion.refs_0_) | copy-start | bytes 786436
  5.9 44.7 %copy-start = (bf16[8,64,1792]{2,1,0:T(8,128)(2,1)S(1)}, bf16[8,64,1792]{2,1,0:T(8,128)(2,1)}, u32[]{:S(2)}) copy-start(bf16[8,64,1792]{2,1,0:T(8,128)(2,1)} %get-tuple-element.73.mine_ref) | copy-start | bytes 5505028
  5.9 17.4 %collective-permute-start.4 = (bf16[8,64,1792]{2,1,0:T(8,128)(2,1)}, bf16[8,64,1792]{2,1,0:T(8,128)(2,1)S(1)}, u32[]{:S(2)}, u32[]{:S(2)}) collective-permute-start(bf16[8,64,1792]{2,1,0:T(8,128)(2,1)} %get-tuple-element.60), channel_id=1, source_target_pairs={{0,1},{1,0},{2,3},{3,2},{4,5},{5,4},{6,7},{7,6},{8,9},{9,8},{10,11... | collective-permute-start | bytes 5505032 | tf_op jit(solution)/shard_map/ppermute | solution.py:462
  6.0 9.5 %collective-permute-start.1 = (bf16[32,4096]{1,0:T(8,128)(2,1)S(1)}, bf16[32,4096]{1,0:T(8,128)(2,1)S(1)}, u32[]{:S(2)}, u32[]{:S(2)}) collective-permute-start(bf16[32,4096]{1,0:T(8,128)(2,1)S(1)} %pad_maximum_fusion.refs_0_), channel_id=1, source_target_pairs={{0,4},{1,5},{4,8},{5,9},{8,12},{9,13},{12,14},{13,15},{14,10},{15,... | collective-permute-start | bytes 786440 | tf_op jit(solution)/shard_map/ppermute | solution.py:411
  9.1 14.2 %collective-permute-start.5 = (bf16[64,4096]{1,0:T(8,128)(2,1)}, bf16[64,4096]{1,0:T(8,128)(2,1)S(1)}, u32[]{:S(2)}, u32[]{:S(2)}) collective-permute-start(bf16[64,4096]{1,0:T(8,128)(2,1)} %get-tuple-element.61), channel_id=1, source_target_pairs={{0,1},{1,0},{2,3},{3,2},{4,5},{5,4},{6,7},{7,6},{8,9},{9,8},{10,11... | collective-permute-start | bytes 1572872 | tf_op jit(solution)/shard_map/ppermute | solution.py:463
  12.5 10.9 %copy-start.10 = (s32[16]{0:T(128)}, s32[16]{0:T(128)S(1)}, u32[]{:S(2)}) copy-start(s32[16]{0:T(128)S(1)} %get-tuple-element.51.begin_ref) | copy-start | bytes 196
  12.5 8.7 %collective-permute-start.2 = (bf16[32,4096]{1,0:T(8,128)(2,1)S(1)}, bf16[32,4096]{1,0:T(8,128)(2,1)S(1)}, u32[]{:S(2)}, u32[]{:S(2)}) collective-permute-start(bf16[32,4096]{1,0:T(8,128)(2,1)S(1)} %pad_maximum_fusion.refs_0_), channel_id=1, source_target_pairs={{4,0},{5,1},{8,4},{9,5},{12,8},{13,9},{14,12},{15,13},{10,14},{11,... | collective-permute-start | bytes 786440 | tf_op jit(solution)/shard_map/ppermute | solution.py:413
  15.5 22.7 %copy-start.13 = (bf16[32,4096]{1,0:T(8,128)(2,1)}, bf16[32,4096]{1,0:T(8,128)(2,1)S(1)}, u32[]{:S(2)}) copy-start(bf16[32,4096]{1,0:T(8,128)(2,1)S(1)} %collective-permute-done.1.refs_1_) | copy-start | bytes 786436
  15.6 7.8 %collective-permute-start.3 = (bf16[32,4096]{1,0:T(8,128)(2,1)S(1)}, bf16[32,4096]{1,0:T(8,128)(2,1)S(1)}, u32[]{:S(2)}, u32[]{:S(2)}) collective-permute-start(bf16[32,4096]{1,0:T(8,128)(2,1)S(1)} %collective-permute-done.1.refs_1_), channel_id=1, source_target_pairs={{0,4},{1,5},{4,8},{5,9},{8,12},{9,13},{12,14},{13,15},{14,10},{15,... | collective-permute-start | bytes 786440 | tf_op jit(solution)/shard_map/ppermute | solution.py:411
  21.2 17.1 %copy-start.14 = (bf16[32,4096]{1,0:T(8,128)(2,1)}, bf16[32,4096]{1,0:T(8,128)(2,1)S(1)}, u32[]{:S(2)}) copy-start(bf16[32,4096]{1,0:T(8,128)(2,1)S(1)} %collective-permute-done.2.refs_2_) | copy-start | bytes 786436
  21.2 8.0 %collective-permute-start.6 = (bf16[32,4096]{1,0:T(8,128)(2,1)S(1)}, bf16[32,4096]{1,0:T(8,128)(2,1)}, u32[]{:S(2)}, u32[]{:S(2)}) collective-permute-start(bf16[32,4096]{1,0:T(8,128)(2,1)S(1)} %collective-permute-done.2.refs_2_), channel_id=1, source_target_pairs={{4,0},{5,1},{8,4},{9,5},{12,8},{13,9},{14,12},{15,13},{10,14},{11,... | collective-permute-start | bytes 786440 | tf_op jit(solution)/shard_map/ppermute | solution.py:413
  23.3 5.9 %copy-start.15 = (bf16[32,4096]{1,0:T(8,128)(2,1)}, bf16[32,4096]{1,0:T(8,128)(2,1)S(1)}, u32[]{:S(2)}) copy-start(bf16[32,4096]{1,0:T(8,128)(2,1)S(1)} %collective-permute-done.3.refs_3_) | copy-start | bytes 786436
  23.3 15.0 %copy-start.12 = (bf16[64,4096]{1,0:T(8,128)(2,1)}, bf16[64,4096]{1,0:T(8,128)(2,1)S(1)}, u32[]{:S(2)}) copy-start(bf16[64,4096]{1,0:T(8,128)(2,1)S(1)} %collective-permute-done.5.refs_9_) | copy-start | bytes 1572868
  23.3 1.3 copy-start.1
  24.6 7.0 %collective-permute-start.7 = (bf16[32,4096]{1,0:T(8,128)(2,1)S(1)}, bf16[32,4096]{1,0:T(8,128)(2,1)}, u32[]{:S(2)}, u32[]{:S(2)}) collective-permute-start(bf16[32,4096]{1,0:T(8,128)(2,1)S(1)} %collective-permute-done.3.refs_3_), channel_id=1, source_target_pairs={{0,4},{1,5},{4,8},{5,9},{8,12},{9,13},{12,14},{13,15},{14,10},{15,... | collective-permute-start | bytes 786440 | tf_op jit(solution)/shard_map/ppermute | solution.py:411
  29.2 7.3 %collective-permute-start.8 = (bf16[32,4096]{1,0:T(8,128)(2,1)}, bf16[32,4096]{1,0:T(8,128)(2,1)}, u32[]{:S(2)}, u32[]{:S(2)}) collective-permute-start(bf16[32,4096]{1,0:T(8,128)(2,1)} %collective-permute-done.6.refs_4_), channel_id=1, source_target_pairs={{4,0},{5,1},{8,4},{9,5},{12,8},{13,9},{14,12},{15,13},{10,14},{11,... | collective-permute-start | bytes 786440 | tf_op jit(solution)/shard_map/ppermute | solution.py:413
  31.6 6.7 %collective-permute-start.9 = (bf16[32,4096]{1,0:T(8,128)(2,1)}, bf16[32,4096]{1,0:T(8,128)(2,1)}, u32[]{:S(2)}, u32[]{:S(2)}) collective-permute-start(bf16[32,4096]{1,0:T(8,128)(2,1)} %collective-permute-done.7.refs_5_), channel_id=1, source_target_pairs={{0,4},{1,5},{4,8},{5,9},{8,12},{9,13},{12,14},{13,15},{14,10},{15,... | collective-permute-start | bytes 786440 | tf_op jit(solution)/shard_map/ppermute | solution.py:411
  32.7 17.9 %copy-start.2 = (bf16[8,64,1792]{2,1,0:T(8,128)(2,1)S(1)}, bf16[8,64,1792]{2,1,0:T(8,128)(2,1)}, u32[]{:S(2)}) copy-start(bf16[8,64,1792]{2,1,0:T(8,128)(2,1)} %copy-done.1) | copy-start | bytes 5505028
  43.5 5.0 %collective-permute-start.10 = (f32[128,128]{1,0:T(8,128)}, f32[128,128]{1,0:T(8,128)S(1)}, u32[]{:S(2)}, u32[]{:S(2)}) collective-permute-start(f32[128,128]{1,0:T(8,128)} %get-tuple-element.64), channel_id=1, source_target_pairs={{0,1},{1,0},{2,3},{3,2},{4,5},{5,4},{6,7},{7,6},{8,9},{9,8},{10,11... | collective-permute-start | bytes 196616 | tf_op jit(solution)/shard_map/ppermute | solution.py:479
  43.6 3.6 %collective-permute-start.11 = (s32[1]{0:T(128)}, s32[1]{0:T(128)}, u32[]{:S(2)}, u32[]{:S(2)}) collective-permute-start(s32[1]{0:T(128)} %get-tuple-element.67), channel_id=1, source_target_pairs={{0,16},{16,0},{1,17},{17,1},{2,18},{18,2},{3,19},{19,3},{4,20},{20... | collective-permute-start | bytes 20 | tf_op jit(solution)/shard_map/ppermute | solution.py:427
  49.4 14.0 %collective-permute-start.15 = (bf16[256,4096]{1,0:T(8,128)(2,1)}, bf16[256,4096]{1,0:T(8,128)(2,1)}, u32[]{:S(2)}, u32[]{:S(2)}) collective-permute-start(bf16[256,4096]{1,0:T(8,128)(2,1)} %get-tuple-element.78), channel_id=1, source_target_pairs={{0,1},{1,0},{2,3},{3,2},{4,5},{5,4},{6,7},{7,6},{8,9},{9,8},{10,11... | collective-permute-start | bytes 6291464 | tf_op jit(solution)/shard_map/ppermute | solution.py:497
  49.5 4.4 %collective-permute-start.12 = (bf16[128,128]{1,0:T(8,128)(2,1)S(1)}, bf16[128,128]{1,0:T(8,128)(2,1)S(1)}, u32[]{:S(2)}, u32[]{:S(2)}) collective-permute-start(bf16[128,128]{1,0:T(8,128)(2,1)S(1)} %multiply_convert_fusion.coeff_ref), channel_id=1, source_target_pairs={{0,2},{1,3},{2,0},{3,1},{4,6},{5,7},{6,4},{7,5},{8,10},{9,11},{10,... | collective-permute-start | bytes 98312 | tf_op jit(solution)/shard_map/ppermute | solution.py:500
  53.9 4.0 %collective-permute-start.13 = (bf16[128,128]{1,0:T(8,128)(2,1)S(1)}, bf16[128,128]{1,0:T(8,128)(2,1)S(1)}, u32[]{:S(2)}, u32[]{:S(2)}) collective-permute-start(bf16[128,128]{1,0:T(8,128)(2,1)S(1)} %add.40), channel_id=1, source_target_pairs={{0,4},{1,5},{2,6},{3,7},{4,0},{5,1},{6,2},{7,3},{8,12},{9,13},{10,... | collective-permute-start | bytes 98312 | tf_op jit(solution)/shard_map/ppermute | solution.py:500
  57.9 4.9 %collective-permute-start.14 = (bf16[128,128]{1,0:T(8,128)(2,1)S(1)}, bf16[128,128]{1,0:T(8,128)(2,1)S(1)}, u32[]{:S(2)}, u32[]{:S(2)}) collective-permute-start(bf16[128,128]{1,0:T(8,128)(2,1)S(1)} %add.41), channel_id=1, source_target_pairs={{0,8},{1,9},{2,10},{3,11},{4,12},{5,13},{6,14},{7,15},{8,0},{9,1},... | collective-permute-start | bytes 98312 | tf_op jit(solution)/shard_map/ppermute | solution.py:500
  63.4 46.1 %all-to-all-start.3 = ((bf16[8,64,1792]{2,1,0:T(8,128)(2,1)}), bf16[8,64,1792]{2,1,0:T(8,128)(2,1)}, u32[]{:S(2)}, u32[]{:S(2)}) async-start(bf16[8,64,1792]{2,1,0:T(8,128)(2,1)} %shard_map.94), calls=%async_computation.3 | async-start | bytes 3670016 | tf_op jit(solution)/shard_map/all_to_all | solution.py:487
  71.1 14.8 %copy-start.3 = (bf16[8,64,1792]{2,1,0:T(8,128)(2,1)S(1)}, bf16[8,64,1792]{2,1,0:T(8,128)(2,1)}, u32[]{:S(2)}) copy-start(bf16[8,64,1792]{2,1,0:T(8,128)(2,1)} %copy-done.1) | copy-start | bytes 5505028
  109.5 1.2 slice-start
  (2 other events, 1.3 us)

commit v2 on v1

--- a/solution.py
+++ b/solution.py
@@ -514,10 +514,10 @@
 
     def later(count):
         def run():
-            value = jnp.zeros((chips, rest - count, up_weight.shape[1]), adapter_up.dtype)
+            value = far
             if count:
                 late = exchange(far[:, :count])
-                value = jnp.concatenate([late, value], axis=1)
+                value = jnp.concatenate([late, far[:, count:]], axis=1)
             return value
 
         return run

time: 145 us -> 138 us (0.952)
  blocking collectives: 26.7 us -> 0 us
  waiting for transfers between devices: 45.3 us -> 58.6 us
  starting transfers between devices: 20.8 us -> 24.2 us
    all_to_all x1 -> x0, blocking collectives: 26.7 us -> none  [exchange(): lax.all_to_all(value, 'tensor', split_axis=0, concat_axis=0, axis_index_g...]
    all_to_all x1 -> x2, waiting for transfers between devices: 20.3 us -> 33.5 us  [exchange(): lax.all_to_all(value, 'tensor', split_axis=0, concat_axis=0, axis_index_g...]
    all_to_all x1 -> x2, starting transfers between devices: 5.22 us -> 8.68 us  [exchange(): lax.all_to_all(value, 'tensor', split_axis=0, concat_axis=0, axis_index_g...]
  transfers between devices with their start and end apart: 17 -> 18, of which waited for: 11 -> 12; matrix products, arithmetic and copies ran while one was open for 13% -> 14% of each run, Pallas kernels for 9% -> 9%
where the time goes in v2:
time: 138 us; the launch traced here: 137 us
  waiting for transfers between devices  58.6 us (42%)
  Pallas kernels  25.8 us (19%)
  starting transfers between devices  24.2 us (18%)
  matrix products  14.8 us (11%)
  local copies, waits for them, and re-layouts  6.9 us (5%)
  other arithmetic  5.4 us (4%)
    all_to_all x2, waiting for transfers between devices, exchange(): lax.all_to_all(value, 'tensor', split_axis=0, concat_axis=0, axis_index_g...  33.5 us
    dot_general x1, matrix products, pooled(): jnp.dot(jnp.concatenate(halves, axis=1), up_weight, preferred_element_typ...  14.8 us
    ppermute x3, waiting for transfers between devices, ring_gather(): held[step] = lax.ppermute(held[step - 1], 'tensor', back)  9.4 us
    all_to_all x2, starting transfers between devices, exchange(): lax.all_to_all(value, 'tensor', split_axis=0, concat_axis=0, axis_index_g...  8.68 us
    ppermute x4, waiting for transfers between devices, ring_gather(): held[-step] = lax.ppermute(held[1 - step], 'tensor', ahead)  8.47 us
    pallas_call x1, Pallas kernels, combine(): pl.pallas_call(kernel, in_specs=[smem] * 2 + [pl.BlockSpec(memory_space=p...  7.59 us
    ppermute x4, starting transfers between devices, ring_gather(): held[-step] = lax.ppermute(held[1 - step], 'tensor', ahead)  7.43 us
    pallas_call x2, Pallas kernels, build_payload(): pl.pallas_call(kernel, in_specs=[pl.BlockSpec(memory_space=pltpu.VMEM)] *...  6.51 us
  transfers between devices with their start and end apart: 18, of which 12 were waited for; matrix products, arithmetic and copies ran while one was open for 14% of the time, Pallas kernels for 9%

profile of v2, /device:TPU:0, one launch (start us, length us, event | category | flops | bytes accessed | tf_op | source)
XLA Modules:
  0.0 137.2 jit_solution(9666542895979915817)
XLA Ops:
  1.5 4.3 %shard_map.92 = (bf16[8,64,1792]{2,1,0:T(8,128)(2,1)}, bf16[8,64,1792]{2,1,0:T(8,128)(2,1)}, bf16[64,4096]{1,0:T(8,128)(2,1)}) custom-call(s32[1]{0:T(128)} %bitcast.2.core_ref, bf16[64,28672]{1,0:T(8,128)(2,1)} %bitcast.10, bf16[64,8192]{1,0:T(8,128)(2,1)} %bitcast.8), custom_call_target="tpu_custom_call" | custom-call | bytes 7340032 | tf_op jit(solution)/shard_map/pallas_call | solution.py:63
  6.0 3.0 %collective-permute-start.1 = (bf16[32,4096]{1,0:T(8,128)(2,1)S(1)}, bf16[32,4096]{1,0:T(8,128)(2,1)S(1)}, u32[]{:S(2)}, u32[]{:S(2)}) collective-permute-start(bf16[32,4096]{1,0:T(8,128)(2,1)S(1)} %pad_maximum_fusion.2.refs_0_), channel_id=1, source_target_pairs={{0,4},{1,5},{4,8},{5,9},{8,12},{9,13},{12,14},{13,15},{14,10},{15,... | collective-permute-start | bytes 786440 | tf_op jit(solution)/shard_map/ppermute | solution.py:411
  9.1 2.1 %shard_map.91 = (f32[128,128]{1,0:T(8,128)S(1)}, f32[128,128]{1,0:T(8,128)S(1)}, bf16[128,256]{1,0:T(8,128)(2,1)S(1)}, f32[128,128]{1,0:T(8,128)S(1)}, bf16[128,...) custom-call(s32[16]{0:T(128)S(1)} %copy-done.5, s32[16]{0:T(128)S(1)} %copy-done.6, ...), custom_call_target="tpu_custom_call" | custom-call | flops 6553600 | bytes 524288 | tf_op jit(solution)/shard_map/pallas_call | solution.py:159
  12.6 3.0 %collective-permute-done.1.refs_1_ = bf16[32,4096]{1,0:T(8,128)(2,1)S(1)} collective-permute-done((bf16[32,4096]{1,0:T(8,128)(2,1)S(1)}, bf16[32,4096]{1,0:T(8,128)(2,1)S(1)}, u32[]{:S(2)}, u32[]{:S(2)}) %collective-permute-start.1) | collective-permute-done | bytes 262176 | tf_op jit(solution)/shard_map/ppermute | solution.py:411
  15.6 1.8 %collective-permute-start.3 = (bf16[32,4096]{1,0:T(8,128)(2,1)S(1)}, bf16[32,4096]{1,0:T(8,128)(2,1)S(1)}, u32[]{:S(2)}, u32[]{:S(2)}) collective-permute-start(bf16[32,4096]{1,0:T(8,128)(2,1)S(1)} %collective-permute-done.1.refs_1_), channel_id=1, source_target_pairs={{0,4},{1,5},{4,8},{5,9},{8,12},{9,13},{12,14},{13,15},{14,10},{15,... | collective-permute-start | bytes 786440 | tf_op jit(solution)/shard_map/ppermute | solution.py:411
  17.3 3.8 %collective-permute-done.2.refs_2_ = bf16[32,4096]{1,0:T(8,128)(2,1)S(1)} collective-permute-done((bf16[32,4096]{1,0:T(8,128)(2,1)S(1)}, bf16[32,4096]{1,0:T(8,128)(2,1)S(1)}, u32[]{:S(2)}, u32[]{:S(2)}) %collective-permute-start.2) | collective-permute-done | bytes 262176 | tf_op jit(solution)/shard_map/ppermute | solution.py:413
  21.5 1.8 %collective-permute-done.3.refs_3_ = bf16[32,4096]{1,0:T(8,128)(2,1)S(1)} collective-permute-done((bf16[32,4096]{1,0:T(8,128)(2,1)S(1)}, bf16[32,4096]{1,0:T(8,128)(2,1)S(1)}, u32[]{:S(2)}, u32[]{:S(2)}) %collective-permute-start.3) | collective-permute-done | bytes 262176 | tf_op jit(solution)/shard_map/ppermute | solution.py:411
  23.3 1.3 copy-done.1
  24.6 1.5 %collective-permute-start.7 = (bf16[32,4096]{1,0:T(8,128)(2,1)S(1)}, bf16[32,4096]{1,0:T(8,128)(2,1)}, u32[]{:S(2)}, u32[]{:S(2)}) collective-permute-start(bf16[32,4096]{1,0:T(8,128)(2,1)S(1)} %collective-permute-done.3.refs_3_), channel_id=1, source_target_pairs={{0,4},{1,5},{4,8},{5,9},{8,12},{9,13},{12,14},{13,15},{14,10},{15,... | collective-permute-start | bytes 786440 | tf_op jit(solution)/shard_map/ppermute | solution.py:411
  26.1 3.1 %collective-permute-done.6.refs_4_ = bf16[32,4096]{1,0:T(8,128)(2,1)} collective-permute-done((bf16[32,4096]{1,0:T(8,128)(2,1)S(1)}, bf16[32,4096]{1,0:T(8,128)(2,1)}, u32[]{:S(2)}, u32[]{:S(2)}) %collective-permute-start.6) | collective-permute-done | bytes 262176 | tf_op jit(solution)/shard_map/ppermute | solution.py:413
  29.6 1.9 %collective-permute-done.7.refs_5_ = bf16[32,4096]{1,0:T(8,128)(2,1)} collective-permute-done((bf16[32,4096]{1,0:T(8,128)(2,1)S(1)}, bf16[32,4096]{1,0:T(8,128)(2,1)}, u32[]{:S(2)}, u32[]{:S(2)}) %collective-permute-start.7) | collective-permute-done | bytes 262176 | tf_op jit(solution)/shard_map/ppermute | solution.py:411
  32.7 1.4 %fusion.4.places_ref = s32[16]{0:T(128)} fusion(s32[16,16]{1,0:T(8,128)} %constant.30.clone, s32[]{:T(128)S(6)} %select_n.24), kind=kLoop, calls=%fused_computation.13 | loop fusion | bytes 132 | tf_op jit(solution)/shard_map/jit(dynamic_index_in_dim)/squeeze | solution.py:420
  34.1 2.4 %collective-permute-done.8.refs_6_ = bf16[32,4096]{1,0:T(8,128)(2,1)} collective-permute-done((bf16[32,4096]{1,0:T(8,128)(2,1)}, bf16[32,4096]{1,0:T(8,128)(2,1)}, u32[]{:S(2)}, u32[]{:S(2)}) %collective-permute-start.8) | collective-permute-done | bytes 262176 | tf_op jit(solution)/shard_map/ppermute | solution.py:413
  36.6 1.7 %collective-permute-done.9.refs_7_ = bf16[32,4096]{1,0:T(8,128)(2,1)} collective-permute-done((bf16[32,4096]{1,0:T(8,128)(2,1)}, bf16[32,4096]{1,0:T(8,128)(2,1)}, u32[]{:S(2)}, u32[]{:S(2)}) %collective-permute-start.9) | collective-permute-done | bytes 262176 | tf_op jit(solution)/shard_map/ppermute | solution.py:411
  38.3 5.3 %shard_map.93 = (bf16[256,4096]{1,0:T(8,128)(2,1)}, f32[128,128]{1,0:T(8,128)}) custom-call(s32[16]{0:T(128)} %fusion.4.places_ref, s32[1]{0:T(128)} %bitcast.2.core_ref, f32[128,128]{1,0:T(8,128)} %copy-done.4, bf16[32,4096]{1,0:T(8,128)(2,1)} %copy-done.12, bf16[32,4096]{1,0:T(8,128)(2,1)} %copy-done.14, bf16[32,4096]{1,0:T(8,128)(2,1)} %copy-done.15, ...), custom_call_target="tpu_custom_call" | custom-call | flops 268435456 | bytes 4194304 | tf_op jit(solution)/shard_map/pallas_call | solution.py:243
  44.8 2.6 %collective-permute-done.11 = s32[1]{0:T(128)} collective-permute-done((s32[1]{0:T(128)}, s32[1]{0:T(128)}, u32[]{:S(2)}, u32[]{:S(2)}) %collective-permute-start.11) | collective-permute-done | bytes 36 | tf_op jit(solution)/shard_map/ppermute | solution.py:427
  50.7 3.3 %shard_map.94 = bf16[8,64,1792]{2,1,0:T(8,128)(2,1)} custom-call(bf16[128,256]{1,0:T(8,128)(2,1)S(1)} %get-tuple-element.83.choose_ref, f32[128,128]{1,0:T(8,128)S(1)} %get-tuple-element.72.live_ref, bf16[128,128]{1,0:T(8,128)(2,1)S(1)} %get-tuple-element.73.fixed_ref, bf16[128,128]{1,0:T(8,128)(2,1)S(1)} %multiply_convert_fusion.coeff_ref, ...), custom_call_target="tpu_custom_call" | custom-call | flops 234881024 | bytes 5505024 | tf_op jit(solution)/shard_map/pallas_call | solution.py:286
  54.0 1.6 %collective-permute-start.13 = (bf16[128,128]{1,0:T(8,128)(2,1)S(1)}, bf16[128,128]{1,0:T(8,128)(2,1)S(1)}, u32[]{:S(2)}, u32[]{:S(2)}) collective-permute-start(bf16[128,128]{1,0:T(8,128)(2,1)S(1)} %add.36), channel_id=1, source_target_pairs={{0,4},{1,5},{2,6},{3,7},{4,0},{5,1},{6,2},{7,3},{8,12},{9,13},{10,... | collective-permute-start | bytes 98312 | tf_op jit(solution)/shard_map/ppermute | solution.py:500
  55.6 2.3 %collective-permute-done.13 = bf16[128,128]{1,0:T(8,128)(2,1)S(1)} collective-permute-done((bf16[128,128]{1,0:T(8,128)(2,1)S(1)}, bf16[128,128]{1,0:T(8,128)(2,1)S(1)}, u32[]{:S(2)}, u32[]{:S(2)}) %collective-permute-start.13) | collective-permute-done | bytes 32800 | tf_op jit(solution)/shard_map/ppermute | solution.py:500
  58.0 2.7 %collective-permute-start.14 = (bf16[128,128]{1,0:T(8,128)(2,1)S(1)}, bf16[128,128]{1,0:T(8,128)(2,1)S(1)}, u32[]{:S(2)}, u32[]{:S(2)}) collective-permute-start(bf16[128,128]{1,0:T(8,128)(2,1)S(1)} %add.37), channel_id=1, source_target_pairs={{0,8},{1,9},{2,10},{3,11},{4,12},{5,13},{6,14},{7,15},{8,0},{9,1},... | collective-permute-start | bytes 98312 | tf_op jit(solution)/shard_map/ppermute | solution.py:500
  60.6 2.2 %collective-permute-done.14 = bf16[128,128]{1,0:T(8,128)(2,1)S(1)} collective-permute-done((bf16[128,128]{1,0:T(8,128)(2,1)S(1)}, bf16[128,128]{1,0:T(8,128)(2,1)S(1)}, u32[]{:S(2)}, u32[]{:S(2)}) %collective-permute-start.14) | collective-permute-done | bytes 32800 | tf_op jit(solution)/shard_map/ppermute | solution.py:500
  63.5 5.2 %all-to-all-start.3 = ((bf16[8,64,1792]{2,1,0:T(8,128)(2,1)}), bf16[8,64,1792]{2,1,0:T(8,128)(2,1)}, u32[]{:S(2)}, u32[]{:S(2)}) async-start(bf16[8,64,1792]{2,1,0:T(8,128)(2,1)} %shard_map.94), calls=%async_computation.3 | async-start | bytes 3670016 | tf_op jit(solution)/shard_map/all_to_all | solution.py:487
  68.7 2.5 %broadcast_select_fusion.1 = (bf16[256,4096]{1,0:T(8,128)(2,1)S(1)}, bf16[256,4096]{1,0:T(8,128)(2,1)S(1)}) fusion(bf16[256,4096]{1,0:T(8,128)(2,1)} %get-tuple-element.79, bf16[256,4096]{1,0:T(8,128)(2,1)} %collective-permute-done.15, pred[]{:T(512)S(6)} %eq.6, pred[]{:T(512)S(6)} %eq.7), kind=kLoop, calls=%fused_computation.7 | loop fusion | flops 2097152 | bytes 8388610 | tf_op jit(solution)/shard_map/jit(_where)/select_n | solution.py:506
  71.2 14.8 %fusion.base_ref = f32[256,1792]{1,0:T(8,128)} fusion(bf16[8192,1792]{1,0:T(8,128)(2,1)} %param.14, bf16[256,4096]{1,0:T(8,128)(2,1)S(1)} %get-tuple-element.93, bf16[256,4096]{1,0:T(8,128)(2,1)S(1)} %get-tuple-element.92), kind=kOutput, calls=%fused_computation.2 | convolution fusion | flops 7524581376 | bytes 35389440 | tf_op jit(solution)/shard_map/dot_general | solution.py:507
  86.0 3.3 %shard_map.95 = bf16[8,64,1792]{2,1,0:T(8,128)(2,1)} custom-call(bf16[128,256]{1,0:T(8,128)(2,1)S(1)} %get-tuple-element.83.choose_ref, f32[128,128]{1,0:T(8,128)S(1)} %get-tuple-element.72.live_ref, bf16[128,128]{1,0:T(8,128)(2,1)S(1)} %get-tuple-element.73.fixed_ref, bf16[128,128]{1,0:T(8,128)(2,1)S(1)} %multiply_convert_fusion.coeff_ref, ...), custom_call_target="tpu_custom_call" | custom-call | flops 234881024 | bytes 5505024 | tf_op jit(solution)/shard_map/pallas_call | solution.py:286
  89.3 20.3 %all-to-all-done.3.incoming_ref = bf16[8,64,1792]{2,1,0:T(8,128)(2,1)} async-done(((bf16[8,64,1792]{2,1,0:T(8,128)(2,1)}), bf16[8,64,1792]{2,1,0:T(8,128)(2,1)}, u32[]{:S(2)}, u32[]{:S(2)}) %all-to-all-start.3) | async-done | bytes 1835040 | tf_op jit(solution)/shard_map/all_to_all | solution.py:487
  109.6 20.0 %conditional.1 = (bf16[8,64,1792]{2,1,0:T(8,128)(2,1)}) conditional(s32[]{:T(128)} %bitcast.5, bf16[8,64,1792]{2,1,0:T(8,128)(2,1)} %shard_map.95, bf16[8,64,1792]{2,1,0:T(8,128)(2,1)} %shard_map.95, bf16[8,64,1792]{2,1,0:T(8,128)(2,1)} %shard_map.95, bf16[8,64,1792]{2,1,0:T(8,128)(2,1)} %shard_map.95), branch_computations={%region_0.1_spmd, %region_1.2_spmd, %region_2.3_spmd, %region_3.4_... | conditional | flops 3670016 | bytes 11010084 | solution.py:527
  109.6 1.9 %slice.8 = bf16[8,16,1792]{2,1,0:T(8,128)(2,1)} slice(bf16[8,64,1792]{2,1,0:T(8,128)(2,1)} %param.1), slice={[0:8], [0:16], [0:1792]} | slice | bytes 917504 | tf_op jit(solution)/shard_map/cond/branch_1_fun/slice | solution.py:519
  111.5 3.5 %all-to-all-start.1 = ((bf16[8,16,1792]{2,1,0:T(8,128)(2,1)}), bf16[8,16,1792]{2,1,0:T(8,128)(2,1)S(1)}, u32[]{:S(2)}, u32[]{:S(2)}) async-start(bf16[8,16,1792]{2,1,0:T(8,128)(2,1)} %slice.8), calls=%async_computation.1 | async-start | bytes 917504 | tf_op jit(solution)/shard_map/cond/branch_1_fun/all_to_all | solution.py:487
  115.0 13.2 %all-to-all-done.1 = bf16[8,16,1792]{2,1,0:T(8,128)(2,1)S(1)} async-done(((bf16[8,16,1792]{2,1,0:T(8,128)(2,1)}), bf16[8,16,1792]{2,1,0:T(8,128)(2,1)S(1)}, u32[]{:S(2)}, u32[]{:S(2)}) %all-to-all-start.1) | async-done | bytes 458784 | tf_op jit(solution)/shard_map/cond/branch_1_fun/all_to_all | solution.py:487
  128.2 1.4 %pad_maximum_fusion = bf16[8,64,1792]{2,1,0:T(8,128)(2,1)} fusion(bf16[8,48,1792]{2,1,0:T(8,128)(2,1)S(1)} %slice-done, bf16[8,16,1792]{2,1,0:T(8,128)(2,1)S(1)} %all-to-all-done.1), kind=kLoop, calls=%fused_computation | loop fusion | flops 3670016 | bytes 3670016 | tf_op jit(solution)/shard_map/cond/branch_1_fun/concatenate | solution.py:520
  129.6 7.6 %shard_map.96 = bf16[256,1792]{1,0:T(8,128)(2,1)} custom-call(s32[16]{0:T(128)} %copy-done.10, s32[1]{0:T(128)S(6)} %max.3.more_ref, f32[256,1792]{1,0:T(8,128)} %fusion.base_ref, s32[256,128]{1,0:T(8,128)} %copy-done.9, bf16[128,128]{1,0:T(8,128)(2,1)} %add.38.coeff_ref, bf16[8,64,1792]{2,1,0:T(8,128)(2,1)} %all-to-all-done.3.incoming_ref, ...), custom_call_target="tpu_custom_call" | custom-call | flops 1879048192 | bytes 6422528 | tf_op jit(solution)/shard_map/pallas_call | solution.py:378
  (56 shorter events, 8.8 us)
Async XLA Ops:
  1.0 4.9 %collective-permute-start = (bf16[16,4096]{1,0:T(8,128)(2,1)S(1)}, bf16[16,4096]{1,0:T(8,128)(2,1)S(1)}, u32[]{:S(2)}, u32[]{:S(2)}) collective-permute-start(bf16[16,4096]{1,0:T(8,128)(2,1)S(1)} %get-tuple-element.95), channel_id=1, source_target_pairs={{0,1},{1,0},{2,3},{3,2},{4,5},{5,4},{6,7},{7,6},{8,9},{9,8},{10,11... | collective-permute-start | bytes 393224 | tf_op jit(solution)/shard_map/ppermute | solution.py:457
  1.5 7.6 %copy-start.5 = (s32[16]{0:T(128)S(1)}, s32[16]{0:T(128)}, u32[]{:S(2)}) copy-start(s32[16]{0:T(128)} %ranks_in.1) | copy-start | bytes 196
  1.5 7.6 %copy-start.6 = (s32[16]{0:T(128)S(1)}, s32[16]{0:T(128)}, u32[]{:S(2)}) copy-start(s32[16]{0:T(128)} %home_in.1) | copy-start | bytes 196
  1.5 7.6 %copy-start.7 = (s32[16]{0:T(128)S(1)}, s32[16]{0:T(128)}, u32[]{:S(2)}) copy-start(s32[16]{0:T(128)} %length_in.1) | copy-start | bytes 196
  1.5 7.6 %copy-start.8 = (s32[16]{0:T(128)S(1)}, s32[16]{0:T(128)}, u32[]{:S(2)}) copy-start(s32[16]{0:T(128)} %adapter_in.1) | copy-start | bytes 196
  5.9 32.4 %copy-start.12 = (bf16[32,4096]{1,0:T(8,128)(2,1)}, bf16[32,4096]{1,0:T(8,128)(2,1)S(1)}, u32[]{:S(2)}) copy-start(bf16[32,4096]{1,0:T(8,128)(2,1)S(1)} %pad_maximum_fusion.2.refs_0_) | copy-start | bytes 786436
  5.9 44.8 %copy-start = (bf16[8,64,1792]{2,1,0:T(8,128)(2,1)S(1)}, bf16[8,64,1792]{2,1,0:T(8,128)(2,1)}, u32[]{:S(2)}) copy-start(bf16[8,64,1792]{2,1,0:T(8,128)(2,1)} %get-tuple-element.74.mine_ref) | copy-start | bytes 5505028
  5.9 17.4 %collective-permute-start.4 = (bf16[8,64,1792]{2,1,0:T(8,128)(2,1)}, bf16[8,64,1792]{2,1,0:T(8,128)(2,1)S(1)}, u32[]{:S(2)}, u32[]{:S(2)}) collective-permute-start(bf16[8,64,1792]{2,1,0:T(8,128)(2,1)} %get-tuple-element.61), channel_id=1, source_target_pairs={{0,1},{1,0},{2,3},{3,2},{4,5},{5,4},{6,7},{7,6},{8,9},{9,8},{10,11... | collective-permute-start | bytes 5505032 | tf_op jit(solution)/shard_map/ppermute | solution.py:462
  6.0 9.5 %collective-permute-start.1 = (bf16[32,4096]{1,0:T(8,128)(2,1)S(1)}, bf16[32,4096]{1,0:T(8,128)(2,1)S(1)}, u32[]{:S(2)}, u32[]{:S(2)}) collective-permute-start(bf16[32,4096]{1,0:T(8,128)(2,1)S(1)} %pad_maximum_fusion.2.refs_0_), channel_id=1, source_target_pairs={{0,4},{1,5},{4,8},{5,9},{8,12},{9,13},{12,14},{13,15},{14,10},{15,... | collective-permute-start | bytes 786440 | tf_op jit(solution)/shard_map/ppermute | solution.py:411
  9.1 14.2 %collective-permute-start.5 = (bf16[64,4096]{1,0:T(8,128)(2,1)}, bf16[64,4096]{1,0:T(8,128)(2,1)S(1)}, u32[]{:S(2)}, u32[]{:S(2)}) collective-permute-start(bf16[64,4096]{1,0:T(8,128)(2,1)} %get-tuple-element.62), channel_id=1, source_target_pairs={{0,1},{1,0},{2,3},{3,2},{4,5},{5,4},{6,7},{7,6},{8,9},{9,8},{10,11... | collective-permute-start | bytes 1572872 | tf_op jit(solution)/shard_map/ppermute | solution.py:463
  12.5 10.8 %copy-start.10 = (s32[16]{0:T(128)}, s32[16]{0:T(128)S(1)}, u32[]{:S(2)}) copy-start(s32[16]{0:T(128)S(1)} %get-tuple-element.52.begin_ref) | copy-start | bytes 196
  12.5 8.7 %collective-permute-start.2 = (bf16[32,4096]{1,0:T(8,128)(2,1)S(1)}, bf16[32,4096]{1,0:T(8,128)(2,1)S(1)}, u32[]{:S(2)}, u32[]{:S(2)}) collective-permute-start(bf16[32,4096]{1,0:T(8,128)(2,1)S(1)} %pad_maximum_fusion.2.refs_0_), channel_id=1, source_target_pairs={{4,0},{5,1},{8,4},{9,5},{12,8},{13,9},{14,12},{15,13},{10,14},{11,... | collective-permute-start | bytes 786440 | tf_op jit(solution)/shard_map/ppermute | solution.py:413
  15.5 22.7 %copy-start.14 = (bf16[32,4096]{1,0:T(8,128)(2,1)}, bf16[32,4096]{1,0:T(8,128)(2,1)S(1)}, u32[]{:S(2)}) copy-start(bf16[32,4096]{1,0:T(8,128)(2,1)S(1)} %collective-permute-done.1.refs_1_) | copy-start | bytes 786436
  15.6 7.8 %collective-permute-start.3 = (bf16[32,4096]{1,0:T(8,128)(2,1)S(1)}, bf16[32,4096]{1,0:T(8,128)(2,1)S(1)}, u32[]{:S(2)}, u32[]{:S(2)}) collective-permute-start(bf16[32,4096]{1,0:T(8,128)(2,1)S(1)} %collective-permute-done.1.refs_1_), channel_id=1, source_target_pairs={{0,4},{1,5},{4,8},{5,9},{8,12},{9,13},{12,14},{13,15},{14,10},{15,... | collective-permute-start | bytes 786440 | tf_op jit(solution)/shard_map/ppermute | solution.py:411
  21.2 17.1 %copy-start.15 = (bf16[32,4096]{1,0:T(8,128)(2,1)}, bf16[32,4096]{1,0:T(8,128)(2,1)S(1)}, u32[]{:S(2)}) copy-start(bf16[32,4096]{1,0:T(8,128)(2,1)S(1)} %collective-permute-done.2.refs_2_) | copy-start | bytes 786436
  21.2 8.0 %collective-permute-start.6 = (bf16[32,4096]{1,0:T(8,128)(2,1)S(1)}, bf16[32,4096]{1,0:T(8,128)(2,1)}, u32[]{:S(2)}, u32[]{:S(2)}) collective-permute-start(bf16[32,4096]{1,0:T(8,128)(2,1)S(1)} %collective-permute-done.2.refs_2_), channel_id=1, source_target_pairs={{4,0},{5,1},{8,4},{9,5},{12,8},{13,9},{14,12},{15,13},{10,14},{11,... | collective-permute-start | bytes 786440 | tf_op jit(solution)/shard_map/ppermute | solution.py:413
  23.3 5.9 %copy-start.16 = (bf16[32,4096]{1,0:T(8,128)(2,1)}, bf16[32,4096]{1,0:T(8,128)(2,1)S(1)}, u32[]{:S(2)}) copy-start(bf16[32,4096]{1,0:T(8,128)(2,1)S(1)} %collective-permute-done.3.refs_3_) | copy-start | bytes 786436
  23.3 15.0 %copy-start.13 = (bf16[64,4096]{1,0:T(8,128)(2,1)}, bf16[64,4096]{1,0:T(8,128)(2,1)S(1)}, u32[]{:S(2)}) copy-start(bf16[64,4096]{1,0:T(8,128)(2,1)S(1)} %collective-permute-done.5.refs_9_) | copy-start | bytes 1572868
  24.6 7.0 %collective-permute-start.7 = (bf16[32,4096]{1,0:T(8,128)(2,1)S(1)}, bf16[32,4096]{1,0:T(8,128)(2,1)}, u32[]{:S(2)}, u32[]{:S(2)}) collective-permute-start(bf16[32,4096]{1,0:T(8,128)(2,1)S(1)} %collective-permute-done.3.refs_3_), channel_id=1, source_target_pairs={{0,4},{1,5},{4,8},{5,9},{8,12},{9,13},{12,14},{13,15},{14,10},{15,... | collective-permute-start | bytes 786440 | tf_op jit(solution)/shard_map/ppermute | solution.py:411
  29.2 7.3 %collective-permute-start.8 = (bf16[32,4096]{1,0:T(8,128)(2,1)}, bf16[32,4096]{1,0:T(8,128)(2,1)}, u32[]{:S(2)}, u32[]{:S(2)}) collective-permute-start(bf16[32,4096]{1,0:T(8,128)(2,1)} %collective-permute-done.6.refs_4_), channel_id=1, source_target_pairs={{4,0},{5,1},{8,4},{9,5},{12,8},{13,9},{14,12},{15,13},{10,14},{11,... | collective-permute-start | bytes 786440 | tf_op jit(solution)/shard_map/ppermute | solution.py:413
  31.6 6.7 %collective-permute-start.9 = (bf16[32,4096]{1,0:T(8,128)(2,1)}, bf16[32,4096]{1,0:T(8,128)(2,1)}, u32[]{:S(2)}, u32[]{:S(2)}) collective-permute-start(bf16[32,4096]{1,0:T(8,128)(2,1)} %collective-permute-done.7.refs_5_), channel_id=1, source_target_pairs={{0,4},{1,5},{4,8},{5,9},{8,12},{9,13},{12,14},{13,15},{14,10},{15,... | collective-permute-start | bytes 786440 | tf_op jit(solution)/shard_map/ppermute | solution.py:411
  32.7 18.0 %copy-start.2 = (bf16[8,64,1792]{2,1,0:T(8,128)(2,1)S(1)}, bf16[8,64,1792]{2,1,0:T(8,128)(2,1)}, u32[]{:S(2)}) copy-start(bf16[8,64,1792]{2,1,0:T(8,128)(2,1)} %copy-done.1) | copy-start | bytes 5505028
  43.6 5.0 %collective-permute-start.10 = (f32[128,128]{1,0:T(8,128)}, f32[128,128]{1,0:T(8,128)S(1)}, u32[]{:S(2)}, u32[]{:S(2)}) collective-permute-start(f32[128,128]{1,0:T(8,128)} %get-tuple-element.65), channel_id=1, source_target_pairs={{0,1},{1,0},{2,3},{3,2},{4,5},{5,4},{6,7},{7,6},{8,9},{9,8},{10,11... | collective-permute-start | bytes 196616 | tf_op jit(solution)/shard_map/ppermute | solution.py:479
  43.6 3.8 %collective-permute-start.11 = (s32[1]{0:T(128)}, s32[1]{0:T(128)}, u32[]{:S(2)}, u32[]{:S(2)}) collective-permute-start(s32[1]{0:T(128)} %get-tuple-element.68), channel_id=1, source_target_pairs={{0,16},{16,0},{1,17},{17,1},{2,18},{18,2},{3,19},{19,3},{4,20},{20... | collective-permute-start | bytes 20 | tf_op jit(solution)/shard_map/ppermute | solution.py:427
  49.5 14.0 %collective-permute-start.15 = (bf16[256,4096]{1,0:T(8,128)(2,1)}, bf16[256,4096]{1,0:T(8,128)(2,1)}, u32[]{:S(2)}, u32[]{:S(2)}) collective-permute-start(bf16[256,4096]{1,0:T(8,128)(2,1)} %get-tuple-element.79), channel_id=1, source_target_pairs={{0,1},{1,0},{2,3},{3,2},{4,5},{5,4},{6,7},{7,6},{8,9},{9,8},{10,11... | collective-permute-start | bytes 6291464 | tf_op jit(solution)/shard_map/ppermute | solution.py:497
  49.5 4.4 %collective-permute-start.12 = (bf16[128,128]{1,0:T(8,128)(2,1)S(1)}, bf16[128,128]{1,0:T(8,128)(2,1)S(1)}, u32[]{:S(2)}, u32[]{:S(2)}) collective-permute-start(bf16[128,128]{1,0:T(8,128)(2,1)S(1)} %multiply_convert_fusion.coeff_ref), channel_id=1, source_target_pairs={{0,2},{1,3},{2,0},{3,1},{4,6},{5,7},{6,4},{7,5},{8,10},{9,11},{10,... | collective-permute-start | bytes 98312 | tf_op jit(solution)/shard_map/ppermute | solution.py:500
  54.0 4.0 %collective-permute-start.13 = (bf16[128,128]{1,0:T(8,128)(2,1)S(1)}, bf16[128,128]{1,0:T(8,128)(2,1)S(1)}, u32[]{:S(2)}, u32[]{:S(2)}) collective-permute-start(bf16[128,128]{1,0:T(8,128)(2,1)S(1)} %add.36), channel_id=1, source_target_pairs={{0,4},{1,5},{2,6},{3,7},{4,0},{5,1},{6,2},{7,3},{8,12},{9,13},{10,... | collective-permute-start | bytes 98312 | tf_op jit(solution)/shard_map/ppermute | solution.py:500
  58.0 4.9 %collective-permute-start.14 = (bf16[128,128]{1,0:T(8,128)(2,1)S(1)}, bf16[128,128]{1,0:T(8,128)(2,1)S(1)}, u32[]{:S(2)}, u32[]{:S(2)}) collective-permute-start(bf16[128,128]{1,0:T(8,128)(2,1)S(1)} %add.37), channel_id=1, source_target_pairs={{0,8},{1,9},{2,10},{3,11},{4,12},{5,13},{6,14},{7,15},{8,0},{9,1},... | collective-permute-start | bytes 98312 | tf_op jit(solution)/shard_map/ppermute | solution.py:500
  63.5 46.1 %all-to-all-start.3 = ((bf16[8,64,1792]{2,1,0:T(8,128)(2,1)}), bf16[8,64,1792]{2,1,0:T(8,128)(2,1)}, u32[]{:S(2)}, u32[]{:S(2)}) async-start(bf16[8,64,1792]{2,1,0:T(8,128)(2,1)} %shard_map.94), calls=%async_computation.3 | async-start | bytes 3670016 | tf_op jit(solution)/shard_map/all_to_all | solution.py:487
  71.2 14.8 %copy-start.3 = (bf16[8,64,1792]{2,1,0:T(8,128)(2,1)S(1)}, bf16[8,64,1792]{2,1,0:T(8,128)(2,1)}, u32[]{:S(2)}) copy-start(bf16[8,64,1792]{2,1,0:T(8,128)(2,1)} %copy-done.1) | copy-start | bytes 5505028
  109.6 18.6 %slice-start = ((bf16[8,64,1792]{2,1,0:T(8,128)(2,1)}), bf16[8,48,1792]{2,1,0:T(8,128)(2,1)S(1)}, s32[]{:S(2)}) async-start(bf16[8,64,1792]{2,1,0:T(8,128)(2,1)} %param.1), calls=%async_computation.4 | async-start | bytes 2752512 | tf_op jit(solution)/shard_map/cond/branch_1_fun/slice | solution.py:520
  111.5 16.7 %all-to-all-start.1 = ((bf16[8,16,1792]{2,1,0:T(8,128)(2,1)}), bf16[8,16,1792]{2,1,0:T(8,128)(2,1)S(1)}, u32[]{:S(2)}, u32[]{:S(2)}) async-start(bf16[8,16,1792]{2,1,0:T(8,128)(2,1)} %slice.8), calls=%async_computation.1 | async-start | bytes 917504 | tf_op jit(solution)/shard_map/cond/branch_1_fun/all_to_all | solution.py:487
  (3 other events, 2.6 us)
